TPU v7x, 256 devices: a whole 4x4x8 slice. The times are simulated.
256 devices in a mesh: replica: 8 (over x, core), fsdp: 32 (over y, z).
Axes of the slice: x: 4, y: 4, z: 8, core: 2. Of those that a mesh axis runs over, the one named last changes fastest.
Arguments:
- delta: bfloat16 [8, 2, 1536, 5120], P('replica', None, 'fsdp'), may hold values from -6 to 6
- error: bfloat16 [8, 2, 1536, 5120], P('replica', None, None, 'fsdp'), may hold values from -6 to 6
- theta: float32 [2, 1536, 5120], P(None, 'fsdp'), may hold values from -6 to 6
- momentum: float32 [2, 1536, 5120], P(None, 'fsdp'), may hold values from -4 to 4
- block_index: int32 [8, 480, 16], P('replica', 'fsdp'), may hold values from 0 to 255, as said below
- block_count: int32 [8, 480], P('replica', 'fsdp'), may hold values from 1 to 16
Outputs:
- theta_new: float32 [2, 1536, 5120], P(None, 'fsdp')
- momentum_new: float32 [2, 1536, 5120], P(None, 'fsdp')
- error_new: bfloat16 [8, 2, 1536, 5120], P('replica', None, None, 'fsdp')
Inputs may be any that keep to these rules, and one draw needn't show every extreme that they name: The first block_count[r, g] entries of each list block_index[r, g, :] are distinct; the remaining entries are padding.
All inputs are finite; a program needn't handle non-finite values.
Results may differ from a plain program's by a relative error of at most 0.0033.
Values may be sent and summed in bfloat16 or wider, within the bound.
A program may use at most 64 MiB of HBM per device.

v0:
```python
import jax
import jax.numpy as jnp
from jax import lax
from jax.sharding import PartitionSpec as P

SPAN = 256


error_decay = 0.95
outer_momentum = 0.9
outer_rate = 0.7


def make_cosines(length):
    freqs = jnp.arange(length, dtype=jnp.float32)[:, None]
    places = jnp.arange(length, dtype=jnp.float32)[None, :]
    angles = jnp.cos(jnp.pi * (2.0 * places + 1.0) * freqs / (2.0 * length))
    scaling = jnp.where(freqs == 0, jnp.sqrt(1.0 / length), jnp.sqrt(2.0 / length))
    return angles * scaling


def spread_blocks(freq_list, values, length):
    onehot = (freq_list[:, :, None] == jnp.arange(length, dtype=jnp.int32)[None, None, :]).astype(
        jnp.float32
    )
    return jnp.einsum(
        "gck,gcn->kgn", onehot, values.astype(jnp.float32), precision=lax.Precision.HIGHEST
    )


def inverse_spans(blocks, cosines, experts, row_count, col_count):
    shaped = blocks.reshape(SPAN, experts, row_count // SPAN, col_count)
    restored = jnp.einsum("kt,kecf->ectf", cosines, shaped, precision=lax.Precision.HIGHEST)
    return restored.reshape(experts, row_count, col_count)


def shards(delta, error, theta, momentum, block_index, block_count):
    cosines = make_cosines(SPAN)
    columns = lax.all_to_all(delta[0], "fsdp", split_axis=2, concat_axis=1, tiled=True)
    carried = error_decay * error[0].astype(jnp.float32) + columns.astype(jnp.float32)
    experts, row_count, col_count = carried.shape
    shaped = carried.reshape(experts, row_count // SPAN, SPAN, col_count)
    spectrum = jnp.einsum("kt,ectf->kecf", cosines, shaped, precision=lax.Precision.HIGHEST)
    freq_list = block_index[0]
    counts = block_count[0]
    groups_here = freq_list.shape[0]
    slot_count = freq_list.shape[1]
    spectrum = spectrum.reshape(SPAN, groups_here, -1)
    live_slots = (jnp.arange(slot_count, dtype=jnp.int32)[None, :] < counts[:, None]).astype(
        jnp.float32
    )
    onehot = (freq_list[:, :, None] == jnp.arange(SPAN, dtype=jnp.int32)[None, None, :]).astype(
        jnp.float32
    )
    picked = (
        jnp.einsum("gck,kgn->gcn", onehot, spectrum, precision=lax.Precision.HIGHEST)
        * live_slots[:, :, None]
    )
    kept_values = lax.optimization_barrier(picked.astype(jnp.bfloat16))
    own_dense = spread_blocks(freq_list, kept_values, SPAN)
    restored = inverse_spans(own_dense, cosines, experts, row_count, col_count)
    error_new = (carried - restored).astype(jnp.bfloat16)[None]
    summed = lax.psum(own_dense.astype(jnp.bfloat16), "replica").astype(jnp.float32)
    averaged = summed / lax.axis_size("replica")
    update_cols = inverse_spans(averaged, cosines, experts, row_count, col_count)
    update = lax.all_to_all(
        update_cols.astype(jnp.bfloat16), "fsdp", split_axis=1, concat_axis=2, tiled=True
    ).astype(update_cols.dtype)
    momentum_new = outer_momentum * momentum + update
    theta_new = theta - outer_rate * (update + outer_momentum * momentum_new)
    return (theta_new, momentum_new, error_new)


def solution(mesh):
    return jax.shard_map(
        shards,
        mesh=mesh,
        in_specs=(
            P("replica", None, "fsdp", None),
            P("replica", None, None, "fsdp"),
            P(None, "fsdp", None),
            P(None, "fsdp", None),
            P("replica", "fsdp", None),
            P("replica", "fsdp"),
        ),
        out_specs=(P(None, "fsdp", None), P(None, "fsdp", None), P("replica", None, None, "fsdp")),
        check_vma=False,
    )
```

profile of v0, /device:TPU:1, one launch (start us, length us, event | category | flops | bytes accessed | tf_op | source)
XLA Modules:
  0.0 221.1 jit_solution(11832168799920592443)
XLA Ops:
  7.2 6.2 %copy.33 = bf16[1,2,48,5120]{2,1,3,0:T(2,128)(2,1)} copy(bf16[1,2,48,5120]{3,2,1,0:T(8,128)(2,1)} %param.6) | data formatting | bytes 1966080 | tf_op args[0]
  13.4 4.2 %bitcast_bitcast_fusion = bf16[5120,2,48]{2,1,0:T(2,128)(2,1)S(1)} fusion(bf16[1,2,48,5120]{2,1,3,0:T(2,128)(2,1)} %copy.33), kind=kLoop, calls=%fused_computation.41 | loop fusion | bytes 1966080
  17.6 4.8 %reshape.101 = bf16[32,2,7680]{2,1,0:T(2,128)(2,1)} reshape(bf16[5120,2,48]{2,1,0:T(2,128)(2,1)S(1)} %bitcast_bitcast_fusion) | data formatting | bytes 1966080
  22.4 12.0 %all-to-all-start = ((bf16[32,2,7680]{2,1,0:T(2,128)(2,1)}), bf16[32,2,7680]{2,1,0:T(2,128)(2,1)S(1)}, u32[]{:S(2)}, u32[]{:S(2)}) async-start(bf16[32,2,7680]{2,1,0:T(2,128)(2,1)} %reshape.101), calls=%async_computation | async-start | bytes 1966080 | tf_op jit(solution)/shard_map/all_to_all | solution.py:39
  34.5 0.2 all-reduce.2.cloned.1.call-start
  34.7 1.6 copy.31
  36.3 2.1 convert_multiply_fusion
  38.4 3.8 %copy.45 = f32[2,6,256,160]{2,1,3,0:T(8,128)} copy(f32[2,6,256,160]{3,2,1,0:T(8,128)} %bitcast.59) | data formatting | bytes 3932160 | tf_op jit(solution)/shard_map/mul | solution.py:40
  42.4 15.6 %all-to-all-done = bf16[32,2,7680]{2,1,0:T(2,128)(2,1)S(1)} async-done(((bf16[32,2,7680]{2,1,0:T(2,128)(2,1)}), bf16[32,2,7680]{2,1,0:T(2,128)(2,1)S(1)}, u32[]{:S(2)}, u32[]{:S(2)}) %all-to-all-start) | async-done | bytes 983072 | tf_op jit(solution)/shard_map/all_to_all | solution.py:39
  58.0 3.7 %reshape.102 = bf16[5120,2,48]{2,1,0:T(2,128)(2,1)} reshape(bf16[32,2,7680]{2,1,0:T(2,128)(2,1)S(1)} %all-to-all-done) | data formatting | bytes 1966080
  61.7 5.6 %copy.34 = f32[2,48,32,160]{3,1,2,0:T(8,128)S(1)} copy(bf16[2,48,32,160]{1,0,3,2:T(2,128)(2,1)} %bitcast.60) | data formatting | bytes 2949120 | tf_op jit(solution)/shard_map/convert_element_type | solution.py:40
  67.3 2.6 %copy.35 = f32[2,6,256,160]{2,1,3,0:T(8,128)} copy(f32[2,6,256,160]{3,2,1,0:T(8,128)S(1)} %bitcast.57) | data formatting | bytes 3932160 | tf_op jit(solution)/shard_map/convert_element_type | solution.py:40
  69.9 2.9 %add_bitcast_fusion = f32[2,6,160,256]{3,1,2,0:T(8,128)S(1)} fusion(f32[2,6,256,160]{2,1,3,0:T(8,128)} %copy.45, f32[2,6,256,160]{2,1,3,0:T(8,128)} %copy.35), kind=kLoop, calls=%fused_computation.5 | loop fusion | flops 491520 | bytes 5898240 | tf_op jit(solution)/shard_map/kt,ectf->kecf/dot_general | solution.py:43
  72.8 0.6 copy.36
  73.4 2.8 %fusion.6 = f32[256,15,128]{2,0,1:T(8,128)S(1)} fusion(f32[15,128,256]{2,1,0:T(8,128)S(1)} %bitcast.62, f32[256]{0:T(256)S(1)} %get-tuple-element.16, f32[256]{0:T(256)S(1)} %get-tuple-element.17), kind=kOutput, calls=%fused_computation.17 | convolution fusion | flops 1510146048 | bytes 3934208 | tf_op jit(solution)/shard_map/kt,ectf->kecf/dot_general | solution.py:43
  76.2 0.8 fusion.3
  77.0 2.1 bitcast_convert_fusion
  79.1 65.9 %all-reduce.2.cloned.1.call-done = bf16[256,15,128]{0,2,1:T(8,128)(2,1)} async-done(((bf16[256,15,128]{0,2,1:T(8,128)(2,1)}), bf16[256,15,128]{0,2,1:T(8,128)(2,1)}) %all-reduce.2.cloned.1.call-update) | async-done | bytes 983056 | tf_op jit(solution)/shard_map/psum | solution.py:63
  144.9 1.4 convert_multiply_fusion.1
  146.4 3.6 %fusion.2 = bf16[2,6,256,160]{2,3,1,0:T(8,128)(2,1)} fusion(f32[256,2,6,160]{0,3,2,1:T(8,128)S(1)} %bitcast.63, f32[256]{0:T(256)S(1)} %get-tuple-element.16, f32[256]{0:T(256)S(1)} %get-tuple-element.17), kind=kOutput, calls=%fused_computation.12 | convolution fusion | flops 1510637568 | bytes 2951168 | tf_op jit(solution)/shard_map/kt,kecf->ectf/dot_general | solution.py:33
  149.9 4.8 %copy.46 = bf16[2,6,256,160]{3,0,2,1:T(2,128)(2,1)} copy(bf16[2,6,256,160]{2,3,1,0:T(8,128)(2,1)} %fusion.2) | data formatting | bytes 1966080 | tf_op jit(solution)/shard_map/convert_element_type | solution.py:67
  154.7 9.9 %all-to-all-start.1 = ((bf16[2,1536,160]{2,0,1:T(2,128)(2,1)}), bf16[2,1536,160]{2,0,1:T(2,128)(2,1)}, u32[]{:S(2)}, u32[]{:S(2)}) async-start(bf16[2,1536,160]{2,0,1:T(2,128)(2,1)} %bitcast.64), calls=%async_computation.1 | async-start | bytes 3145728 | tf_op jit(solution)/shard_map/all_to_all | solution.py:66
  164.6 5.5 %convolution_bitcast_fusion = f32[2,6,256,160]{2,3,1,0:T(8,128)} fusion(f32[256,2,6,160]{0,3,2,1:T(8,128)} %bitcast.61, f32[256]{0:T(256)S(1)} %get-tuple-element.16, f32[256]{0:T(256)S(1)} %get-tuple-element.17), kind=kOutput, calls=%fused_computation.10 | convolution fusion | flops 1510146048 | bytes 3934208 | tf_op jit(solution)/shard_map/kt,kecf->ectf/dot_general | solution.py:33
  170.1 3.3 %copy.47 = f32[2,6,256,160]{3,2,1,0:T(8,128)} copy(f32[2,6,256,160]{2,3,1,0:T(8,128)} %convolution_bitcast_fusion) | data formatting | bytes 3932160 | tf_op jit(solution)/shard_map/reshape | solution.py:34
  173.4 4.1 %fusion.1 = bf16[1,2,1536,160]{3,2,1,0:T(8,128)(2,1)} fusion(f32[1,2,1536,160]{3,2,1,0:T(8,128)} %bitcast.58, f32[2,48,32,160]{3,1,2,0:T(8,128)S(1)} %copy.34, bf16[1,2,1536,160]{3,2,1,0:T(8,128)(2,1)} %copy-done), kind=kLoop, calls=%fused_computation.2 | loop fusion | flops 2457600 | bytes 5898240 | tf_op jit(solution)/shard_map/convert_element_type | solution.py:62
  177.6 2.4 %copy.43 = bf16[1,2,1536,160]{2,3,1,0:T(8,128)(2,1)} copy(bf16[1,2,1536,160]{3,2,1,0:T(8,128)(2,1)} %fusion.1) | data formatting | bytes 1966080
  180.0 20.5 %all-to-all-done.1 = bf16[2,1536,160]{2,0,1:T(2,128)(2,1)} async-done(((bf16[2,1536,160]{2,0,1:T(2,128)(2,1)}), bf16[2,1536,160]{2,0,1:T(2,128)(2,1)}, u32[]{:S(2)}, u32[]{:S(2)}) %all-to-all-start.1) | async-done | bytes 983072 | tf_op jit(solution)/shard_map/all_to_all | solution.py:66
  200.5 1.6 copy.39
  202.1 0.4 convert_bitcast_fusion
  202.5 3.5 %copy.40 = f32[2,48,32,160]{3,2,1,0:T(8,128)} copy(f32[2,48,32,160]{3,1,2,0:T(8,128)S(1)} %convert_bitcast_fusion) | data formatting | bytes 3932160 | tf_op jit(solution)/shard_map/convert_element_type | solution.py:68
  206.0 3.5 %reshape.94 = f32[2,48,5120]{2,1,0:T(8,128)S(1)} reshape(f32[2,48,32,160]{3,2,1,0:T(8,128)} %copy.40) | data formatting | bytes 3932160 | tf_op jit(solution)/shard_map/convert_element_type | solution.py:68
  209.5 4.7 %multiply_subtract_fusion = (f32[2,48,5120]{2,1,0:T(8,128)}, f32[2,48,5120]{2,1,0:T(8,128)}) fusion(f32[2,48,5120]{2,1,0:T(8,128)} %param.8, f32[2,48,5120]{2,1,0:T(8,128)S(1)} %reshape.94, f32[2,48,5120]{2,1,0:T(8,128)} %param.9), kind=kLoop, calls=%fused_computation.7 | loop fusion | flops 2949120 | bytes 9830400 | tf_op jit(solution)/shard_map/sub | solution.py:70
  (10 shorter events, 0.1 us)
Async XLA Ops:
  22.4 35.6 %all-to-all-start = ((bf16[32,2,7680]{2,1,0:T(2,128)(2,1)}), bf16[32,2,7680]{2,1,0:T(2,128)(2,1)S(1)}, u32[]{:S(2)}, u32[]{:S(2)}) async-start(bf16[32,2,7680]{2,1,0:T(2,128)(2,1)} %reshape.101), calls=%async_computation | async-start | bytes 1966080 | tf_op jit(solution)/shard_map/all_to_all | solution.py:39
  34.5 110.5 %all-reduce.2.cloned.1.call-start = ((), (), s32[]{:S(2)}) async-start(), calls=%async_computation.2 | async-start | bytes 1966080 | tf_op jit(solution)/shard_map/psum | solution.py:63
  36.3 2.1 copy-start
  38.4 3.8 %copy-start.1 = (s32[1,15,16]{2,0,1:T(1,128)S(1)}, s32[1,15,16]{2,0,1:T(1,128)}, u32[]{:S(2)}) copy-start(s32[1,15,16]{2,0,1:T(1,128)} %param.10) | copy-start | bytes 2884
  38.4 3.9 %copy-start.2 = (s32[1,15]{1,0:T(1,128)S(1)}, s32[1,15]{1,0:T(1,128)}, u32[]{:S(2)}) copy-start(s32[1,15]{1,0:T(1,128)} %param.11) | copy-start | bytes 184
  154.7 45.7 %all-to-all-start.1 = ((bf16[2,1536,160]{2,0,1:T(2,128)(2,1)}), bf16[2,1536,160]{2,0,1:T(2,128)(2,1)}, u32[]{:S(2)}, u32[]{:S(2)}) async-start(bf16[2,1536,160]{2,0,1:T(2,128)(2,1)} %bitcast.64), calls=%async_computation.1 | async-start | bytes 3145728 | tf_op jit(solution)/shard_map/all_to_all | solution.py:66
Sparse Core Ops, SparseCore 0:
  79.2 65.7 all-reduce.1
where the time goes:
time: 225 us; the launch traced here: 221 us
  waiting for transfers between devices  102 us (45%)
  local copies, waits for them, and re-layouts  52.3 us (23%)
  starting transfers between devices  22.2 us (10%)
  other arithmetic  15.7 us (7%)
  matrix products  14.7 us (7%)
  between operations  14.1 us (6%)
    psum x1, waiting for transfers between devices, shards(): lax.psum(own_dense.astype(jnp.bfloat16), 'replica').astype(jnp.float32)  65.9 us
    unnamed x13, local copies, waits for them, and re-layouts  23 us
    all_to_all x1, waiting for transfers between devices, shards(): lax.all_to_all(update_cols.astype(jnp.bfloat16), 'fsdp', split_axis=1, co...  20.5 us
    all_to_all x1, waiting for transfers between devices, shards(): lax.all_to_all(delta[0], 'fsdp', split_axis=2, concat_axis=1, tiled=True)  15.6 us
    all_to_all x1, starting transfers between devices, shards(): lax.all_to_all(delta[0], 'fsdp', split_axis=2, concat_axis=1, tiled=True)  12 us
    all_to_all x1, starting transfers between devices, shards(): lax.all_to_all(update_cols.astype(jnp.bfloat16), 'fsdp', split_axis=1, co...  9.9 us
    dot_general x2, matrix products, inverse_spans(): jnp.einsum('kt,kecf->ectf', cosines, shaped, precision=lax.Precision.HIGH...  9.03 us
    convert_element_type x2, local copies, waits for them, and re-layouts, shards(): columns.astype(jnp.float32)  8.22 us
  transfers between devices with their start and end apart: 3, of which 3 were waited for; matrix products, arithmetic and copies ran while one was open for 10% of the time, Pallas kernels for 0%

commit v1 on v0

v1 whole, which is shorter than its diff:
```python
import jax
import jax.numpy as jnp
import numpy as np
from jax import lax
from jax.experimental import pallas as pl
from jax.experimental.pallas import tpu as pltpu
from jax.sharding import PartitionSpec as P

SPAN = 256
N = 32
R = 8
ROWS = 48
MESH = pl.DeviceIdType.MESH
F32 = jnp.float32
BF16 = jnp.bfloat16
I32 = jnp.int32


def cosine_parts():
    k = np.arange(SPAN, dtype=np.float64)[:, None]
    t = np.arange(SPAN, dtype=np.float64)[None, :]
    m = np.cos(np.pi * (2.0 * t + 1.0) * k / (2.0 * SPAN))
    m = m * np.where(k == 0, np.sqrt(1.0 / SPAN), np.sqrt(2.0 / SPAN))
    hi = m.astype(jnp.bfloat16)
    lo = (m - hi.astype(np.float64)).astype(jnp.bfloat16)
    return np.stack([hi, lo, hi.T, lo.T])


def div(a, b):
    return lax.div(a, jnp.int32(b))


def rem(a, b):
    return lax.rem(a, jnp.int32(b))


def owner_of(f):
    y, z = div(f, 8), rem(f, 8)
    return 2 * rem(y + z, 4) + div(z, 4)


def dot_nt(a, b):
    return lax.dot_general(a, b, (((1,), (1,)), ((), ())), preferred_element_type=F32)


def dot_tn(a, b):
    return lax.dot_general(a, b, (((0,), (0,)), ((), ())), preferred_element_type=F32)


def dot(a, b):
    return jnp.dot(a, b, preferred_element_type=F32)


def lanes(shape):
    return lax.broadcasted_iota(I32, shape, len(shape) - 1)


def exchange_kernel(
    delta, err, cos, own_idx, flat_idx,
    upd, upd_tail, err_out,
    d_v, e_v, cos_v, send, send_t, recv, recv_t, x_t, low, basis,
    idx_all, kept, kept_all, u_out, u_tail, u_msg, u_recv,
    load_sem, a2a_s, a2a_r, idx_s, idx_r, kept_s, kept_r, upd_s, upd_r, fwd_s, fwd_r,
):
    r = lax.axis_index("replica")
    f = lax.axis_index("fsdp")
    y, z = div(f, 8), rem(f, 8)
    fm = rem(f, 4)
    own = owner_of(f)
    is_owner = r == own

    loads = [
        pltpu.make_async_copy(delta.at[0], d_v.at[0], load_sem.at[0]),
        pltpu.make_async_copy(delta.at[1], d_v.at[1], load_sem.at[1]),
        pltpu.make_async_copy(cos, cos_v, load_sem.at[2]),
        pltpu.make_async_copy(err, e_v, load_sem.at[3]),
    ]
    for c in loads:
        c.start()

    bar = pltpu.get_barrier_semaphore()

    def greet_row(o, _):
        pl.semaphore_signal(bar, inc=1, device_id=(r, rem(f + o, N)), device_id_type=MESH)
        return 0

    def greet_col(o, _):
        pl.semaphore_signal(bar, inc=1, device_id=(rem(r + o, R), f), device_id_type=MESH)
        return 0

    lax.fori_loop(1, N, greet_row, 0)
    lax.fori_loop(1, R, greet_col, 0)

    lane16 = lanes((16, 128))

    def pack_main(e):
        def body(q, _):
            for i in range(3):
                rows = pl.ds(16 * i, 16)
                t = [
                    d_v[e, rows, pl.ds(pl.multiple_of(640 * q + 128 * k, 128), 128)]
                    for k in range(5)
                ]
                send[e, 4 * q, rows] = t[0]
                send[e, 4 * q + 1, rows] = jnp.where(lane16 >= 32, t[1], t[2])
                send[e, 4 * q + 2, rows] = jnp.where(lane16 >= 64, t[2], t[3])
                send[e, 4 * q + 3, rows] = jnp.where(lane16 >= 96, t[3], t[4])
            return 0

        lax.fori_loop(0, 8, body, 0)

    def pack_tail():
        def body(q, _):
            zs = []
            for g in range(6):
                e, i = g // 3, g % 3
                t = [
                    d_v[e, 16 * i:16 * i + 16, pl.ds(pl.multiple_of(640 * q + 128 * k, 128), 128)]
                    for k in range(1, 5)
                ]
                v = jnp.where(
                    lane16 < 32, t[0], jnp.where(lane16 < 64, t[1], jnp.where(lane16 < 96, t[2], t[3]))
                )
                zs.append(v.astype(F32))
            for m in range(4):
                w = [None, None]
                for g in range(6):
                    k = g % 4
                    s = (32 * (k - m)) % 128
                    v = pltpu.roll(zs[g], s, 1) if s else zs[g]
                    p = w[g // 4]
                    w[g // 4] = v if p is None else jnp.where(lane16 < 32 * k, p, v)
                send_t[4 * q + m, 0:16] = w[0].astype(BF16)
                send_t[4 * q + m, 16:32] = w[1].astype(BF16)
            return 0

        lax.fori_loop(0, 8, body, 0)

    def send_main(e):
        def body(o, _):
            d = rem(f + o, N)
            pltpu.make_async_remote_copy(
                src_ref=send.at[e, d],
                dst_ref=recv.at[e, pl.ds(pl.multiple_of(ROWS * f, 16), ROWS)],
                send_sem=a2a_s.at[e], recv_sem=a2a_r.at[e],
                device_id=(r, d), device_id_type=MESH,
            ).start()
            return 0

        lax.fori_loop(1, N, body, 0)

    def send_tail():
        def body(o, _):
            d = rem(f + o, N)
            pltpu.make_async_remote_copy(
                src_ref=send_t.at[d], dst_ref=recv_t.at[f],
                send_sem=a2a_s.at[2], recv_sem=a2a_r.at[2],
                device_id=(r, d), device_id_type=MESH,
            ).start()
            return 0

        lax.fori_loop(1, N, body, 0)

    loads[0].wait()
    pack_main(0)
    pl.semaphore_wait(bar, N - 1 + R - 1)
    send_main(0)
    loads[1].wait()
    pack_main(1)
    send_main(1)
    pack_tail()
    send_tail()
    for e in range(2):
        recv[e, pl.ds(pl.multiple_of(ROWS * f, 16), ROWS)] = send[e, f]
    recv_t[f] = send_t[f]

    def idx_copy():
        return pltpu.make_async_remote_copy(
            src_ref=own_idx, dst_ref=idx_all.at[r],
            send_sem=idx_s, recv_sem=idx_r, device_id=(own, f), device_id_type=MESH,
        )

    @pl.when(jnp.logical_not(is_owner))
    def _():
        idx_copy().start()

    loads[2].wait()
    pick = (lax.broadcasted_iota(I32, (SPAN, SPAN), 0) == flat_idx[0:1, :]).astype(F32)
    pick = jnp.transpose(pick).astype(BF16)
    for part in range(2):
        rows = dot(pick, cos_v[part]).astype(BF16)
        for g in range(15):
            low[32 * g + 16 * part:32 * g + 16 * part + 16] = rows[16 * g:16 * g + 16]

    @pl.when(is_owner)
    def _():
        idx_all[r] = own_idx[...]
        pltpu.make_async_copy(idx_all.at[pl.ds(0, R - 1)], idx_all.at[pl.ds(0, R - 1)], idx_r).wait()
        merged = idx_all[0]
        for p in range(1, R):
            merged = jnp.where(lane16 < 16 * p, merged, idx_all[p])
        kk = lax.broadcasted_iota(I32, (SPAN, 128), 0)
        for g in range(15):
            hot = (kk == merged[g:g + 1, :]).astype(F32).astype(BF16)
            basis[g, :, 0:128] = dot(cos_v[2], hot).astype(BF16)
            basis[g, :, 128:256] = dot(cos_v[3], hot).astype(BF16)

    loads[3].wait()

    place16 = rem(lane16 - 32 * fm + 128, 128)
    place128 = rem(lanes((128, 128)) - 32 * fm + 128, 128)

    def turned(e, c):
        return jnp.concatenate(
            [
                e_v[e, pl.ds(pl.multiple_of(32 * rem(i - fm + 4, 4), 32), 32), SPAN * c:SPAN * c + SPAN]
                for i in range(4)
            ],
            axis=0,
        )

    def main_tiles(e):
        pltpu.make_async_copy(
            recv.at[e, pl.ds(0, (N - 1) * ROWS)], recv.at[e, pl.ds(0, (N - 1) * ROWS)], a2a_r.at[e]
        ).wait()
        for c in range(6):
            b = 6 * e + c
            ga, limit = (5 * b) // 4, 128 - 32 * (b % 4)
            x = recv[e, SPAN * c:SPAN * c + SPAN]
            er = turned(e, c)
            rows = low[32 * ga:32 * ga + 64]
            o = dot(rows, x) + 0.95 * dot_nt(rows, er)
            pa, pb = o[0:16] + o[16:32], o[32:48] + o[48:64]
            first = place16 < limit
            ka = jnp.where(first, pa, 0.0).astype(BF16)
            kb = jnp.where(first, 0.0, pb).astype(BF16)
            kept[b] = ka + kb
            back = dot_tn(jnp.concatenate([ka, ka, kb, kb], axis=0), rows)
            en = 0.95 * er.astype(F32) + jnp.transpose(x.astype(F32)) - back
            en = en.astype(BF16)
            for i in range(4):
                err_out[
                    e, pl.ds(pl.multiple_of(32 * rem(i - fm + 4, 4), 32), 32), SPAN * c:SPAN * c + SPAN
                ] = en[32 * i:32 * i + 32]

    def tail_tiles():
        pltpu.make_async_copy(
            recv_t.at[pl.ds(0, N - 1)], recv_t.at[pl.ds(0, N - 1)], a2a_r.at[2]
        ).wait()
        for tb in range(3):
            for t16 in range(16):
                v = None
                for j in range(4):
                    b = 4 * tb + j
                    e, row = b // 6, SPAN * (b % 6) + 16 * t16
                    s, g = row // ROWS, 3 * e + (row % ROWS) // 16
                    w = recv_t[s, 16 * (g // 4):16 * (g // 4) + 16].astype(F32)
                    sh = (32 * (j - g)) % 128
                    w = pltpu.roll(w, sh, 1) if sh else w
                    v = w if v is None else jnp.where(lane16 < 32 * j, v, w)
                x_t[tb, 16 * t16:16 * t16 + 16] = v.astype(BF16)
        for tb in range(3):
            x = x_t[tb]
            er = jnp.concatenate(
                [
                    e_v[(4 * tb + j) // 6, 128:160, SPAN * ((4 * tb + j) % 6):SPAN * ((4 * tb + j) % 6) + SPAN]
                    for j in range(4)
                ],
                axis=0,
            )
            base = 32 * (5 * tb + 1)
            rows = low[base:base + 128]
            o = dot(rows, x) + 0.95 * dot_nt(rows, er)
            ks = []
            total = None
            for j in range(4):
                p = o[32 * j:32 * j + 16] + o[32 * j + 16:32 * j + 32]
                k = jnp.where(lane16 // 32 == j, p, 0.0).astype(BF16)
                ks += [k, k]
                total = k if total is None else total + k
            kept[12 + tb] = total
            back = dot_tn(jnp.concatenate(ks, axis=0), rows)
            en = 0.95 * er.astype(F32) + jnp.transpose(x.astype(F32)) - back
            en = en.astype(BF16)
            for j in range(4):
                e, c = (4 * tb + j) // 6, (4 * tb + j) % 6
                err_out[e, 128:160, SPAN * c:SPAN * c + SPAN] = en[32 * j:32 * j + 32]

    FIRST, COUNT = (0, 6, 12), (6, 6, 3)

    def kept_copy(p):
        tiles = pl.ds(FIRST[p], COUNT[p])
        return pltpu.make_async_remote_copy(
            src_ref=kept.at[tiles],
            dst_ref=kept_all.at[tiles, pl.ds(pl.multiple_of(16 * r, 16), 16)],
            send_sem=kept_s.at[p], recv_sem=kept_r.at[p],
            device_id=(own, f), device_id_type=MESH,
        )

    def send_kept(p):
        @pl.when(jnp.logical_not(is_owner))
        def _():
            kept_copy(p).start()

    def take_kept(p):
        for b in range(FIRST[p], FIRST[p] + COUNT[p]):
            kept_all[b, pl.ds(pl.multiple_of(16 * r, 16), 16)] = kept[b]
        part = kept_all.at[pl.ds(0, COUNT[p]), pl.ds(0, 16 * (R - 1))]
        pltpu.make_async_copy(part, part, kept_r.at[p]).wait()

    def upd_main_copy(e, d):
        return pltpu.make_async_remote_copy(
            src_ref=u_out.at[e, pl.ds(pl.multiple_of(ROWS * d, 16), ROWS)],
            dst_ref=upd.at[e, r, y],
            send_sem=upd_s.at[e], recv_sem=upd_r.at[e],
            device_id=(r, d), device_id_type=MESH,
        )

    def average_main(e):
        @pl.when(is_owner)
        def _():
            take_kept(e)
            for c in range(6):
                b = 6 * e + c
                ga, limit = (5 * b) // 4, 128 - 32 * (b % 4)
                k = kept_all[b]
                if limit == 128:
                    u = dot(basis[ga], jnp.concatenate([k, k], axis=0))
                else:
                    zero = jnp.zeros_like(k)
                    first = place128 < limit
                    ka = jnp.where(first, k, zero)
                    kb = jnp.where(first, zero, k)
                    u = dot(basis[ga], jnp.concatenate([ka, ka], axis=0))
                    u = u + dot(basis[ga + 1], jnp.concatenate([kb, kb], axis=0))
                u_out[e, SPAN * c:SPAN * c + SPAN] = (u * 0.125).astype(BF16)

            def body(o, _):
                upd_main_copy(e, rem(f + o, N)).start()
                return 0

            lax.fori_loop(1, N, body, 0)
            upd[e, r, y] = u_out[e, pl.ds(pl.multiple_of(ROWS * f, 16), ROWS)]

    def average_tail():
        @pl.when(is_owner)
        def _():
            take_kept(2)
            for tb in range(3):
                k = kept_all[12 + tb]
                u = None
                for j in range(4):
                    kj = jnp.where(lanes((128, 128)) // 32 == j, k, jnp.zeros_like(k))
                    v = dot(basis[5 * tb + 1 + j], jnp.concatenate([kj, kj], axis=0))
                    u = v if u is None else u + v
                u_tail[tb] = u * 0.125
            for d in range(N):
                w = [None, None]
                for g in range(6):
                    e, row = g // 3, ROWS * d + 16 * (g % 3)
                    b = 6 * e + row // SPAN
                    v = u_tail[b // 4, row % SPAN:row % SPAN + 16]
                    sh = (32 * (g - b)) % 128
                    v = pltpu.roll(v, sh, 1) if sh else v
                    p = w[g // 4]
                    w[g // 4] = v if p is None else jnp.where(lane16 < 32 * (g % 4), p, v)
                u_msg[d, 0:16] = w[0].astype(BF16)
                u_msg[d, 16:32] = w[1].astype(BF16)

            def body(o, _):
                d = rem(f + o, N)
                pltpu.make_async_remote_copy(
                    src_ref=u_msg.at[d], dst_ref=u_recv.at[y],
                    send_sem=upd_s.at[2], recv_sem=upd_r.at[2],
                    device_id=(r, d), device_id_type=MESH,
                ).start()
                return 0

            lax.fori_loop(1, N, body, 0)
            u_recv[y] = u_msg[f]

    def wait_upd(p):
        def some(count):
            part = upd.at[p, 0, pl.ds(0, count)] if p < 2 else u_recv.at[pl.ds(0, count)]
            pltpu.make_async_copy(part, part, upd_r.at[p]).wait()

        @pl.when(is_owner)
        def _():
            some(3)

        @pl.when(jnp.logical_not(is_owner))
        def _():
            some(4)

    def fwd_copy(p, other):
        ref = upd.at[p, r] if p < 2 else upd_tail.at[r]
        return pltpu.make_async_remote_copy(
            src_ref=ref, dst_ref=ref, send_sem=fwd_s.at[p], recv_sem=fwd_r.at[p],
            device_id=(other, f), device_id_type=MESH,
        )

    def forward(p):
        wait_upd(p)
        if p == 2:
            x, core = div(r, 2), rem(r, 2)
            tails = [jnp.zeros((16, 128), F32) for _ in range(6)]
            for yy in range(4):
                m = rem(x - yy + 4, 4)
                for g in range(6):
                    v = u_recv[yy, 16 * (g // 4):16 * (g // 4) + 16].astype(F32)
                    v = pltpu.roll(v, rem(32 * (m - g % 4) + 128, 128), 1)
                    tails[g] = jnp.where(div(lane16, 32) == m, v, tails[g])
            for g in range(6):
                upd_tail[r, 16 * g:16 * g + 16] = tails[g].astype(BF16)
        for o in range(1, R):
            fwd_copy(p, rem(r + o, R)).start()

    main_tiles(0)
    send_kept(0)
    average_main(0)
    main_tiles(1)
    send_kept(1)
    forward(0)
    average_main(1)
    tail_tiles()
    send_kept(2)
    forward(1)
    average_tail()
    forward(2)

    for p in range(3):
        part = upd.at[p, pl.ds(0, R - 1)] if p < 2 else upd_tail.at[pl.ds(0, R - 1)]
        pltpu.make_async_copy(part, part, fwd_r.at[p]).wait()
        pltpu.make_async_copy(part, part, fwd_s.at[p]).wait()
        part = send.at[p, pl.ds(0, N - 1)] if p < 2 else send_t.at[pl.ds(0, N - 1)]
        pltpu.make_async_copy(part, part, a2a_s.at[p]).wait()

    @pl.when(is_owner)
    def _():
        for p in range(3):
            part = u_out.at[p, pl.ds(0, ROWS * (N - 1))] if p < 2 else u_msg.at[pl.ds(0, N - 1)]
            pltpu.make_async_copy(part, part, upd_s.at[p]).wait()

    @pl.when(jnp.logical_not(is_owner))
    def _():
        idx_copy().wait_send()
        for p in range(3):
            kept_copy(p).wait_send()


def exchange(delta, err, cos, own_idx, flat_idx):
    vmem = pl.BlockSpec(memory_space=pltpu.VMEM)
    hbm = pl.BlockSpec(memory_space=pl.ANY)
    return pl.pallas_call(
        exchange_kernel,
        out_shape=(
            pltpu.VMEM((2, R, 4, ROWS, 128), BF16),
            pltpu.VMEM((R, 2 * ROWS, 128), BF16),
            pltpu.VMEM((2, 160, 1536), BF16),
        ),
        in_specs=[hbm, hbm, hbm, vmem, vmem],
        out_specs=(vmem, vmem, vmem),
        scratch_shapes=[
            pltpu.VMEM((2, ROWS, 5120), BF16),
            pltpu.VMEM((2, 160, 1536), BF16),
            pltpu.VMEM((4, SPAN, SPAN), BF16),
            pltpu.VMEM((2, N, ROWS, 128), BF16),
            pltpu.VMEM((N, 32, 128), BF16),
            pltpu.VMEM((2, N * ROWS, 128), BF16),
            pltpu.VMEM((N, 32, 128), BF16),
            pltpu.VMEM((3, SPAN, 128), BF16),
            pltpu.VMEM((15 * 32, SPAN), BF16),
            pltpu.VMEM((15, SPAN, SPAN), BF16),
            pltpu.VMEM((R, 16, 128), I32),
            pltpu.VMEM((15, 16, 128), BF16),
            pltpu.VMEM((15, 128, 128), BF16),
            pltpu.VMEM((2, N * ROWS, 128), BF16),
            pltpu.VMEM((3, SPAN, 128), F32),
            pltpu.VMEM((N, 32, 128), BF16),
            pltpu.VMEM((4, 32, 128), BF16),
            pltpu.SemaphoreType.DMA((4,)),
            pltpu.SemaphoreType.DMA((3,)),
            pltpu.SemaphoreType.DMA((3,)),
            pltpu.SemaphoreType.DMA,
            pltpu.SemaphoreType.DMA,
            pltpu.SemaphoreType.DMA((3,)),
            pltpu.SemaphoreType.DMA((3,)),
            pltpu.SemaphoreType.DMA((3,)),
            pltpu.SemaphoreType.DMA((3,)),
            pltpu.SemaphoreType.DMA((3,)),
            pltpu.SemaphoreType.DMA((3,)),
        ],
        compiler_params=pltpu.CompilerParams(
            collective_id=0, has_side_effects=True, vmem_limit_bytes=32 << 20
        ),
        name="exchange",
    )(delta, err, cos, own_idx, flat_idx)


def finish_kernel(
    upd, upd_tail, err, theta, momentum,
    theta_out, momentum_out, err_out,
    th, mo, err_sem, th_sem, mo_sem, th_out_sem, mo_out_sem,
):
    moved = pltpu.make_async_copy(err, err_out, err_sem)
    moved.start()

    def piece(q):
        return pl.ds(pl.multiple_of(640 * q, 128), 640)

    def read(q):
        return (
            pltpu.make_async_copy(theta.at[:, :, piece(q)], th.at[:, :, piece(q)], th_sem.at[q]),
            pltpu.make_async_copy(momentum.at[:, :, piece(q)], mo.at[:, :, piece(q)], mo_sem.at[q]),
        )

    def write(q):
        return (
            pltpu.make_async_copy(th.at[:, :, piece(q)], theta_out.at[:, :, piece(q)], th_out_sem.at[q]),
            pltpu.make_async_copy(mo.at[:, :, piece(q)], momentum_out.at[:, :, piece(q)], mo_out_sem.at[q]),
        )

    for q in range(8):
        for c in read(q):
            c.start()
    lane = lanes((ROWS, 128))
    for q in range(8):
        for c in read(q):
            c.wait()
        y, core = q // 2, q % 2
        reps = [2 * ((y + m) % 4) + core for m in range(4)]
        for e in range(2):
            main = [upd[e, reps[m], y].astype(F32) for m in range(4)]
            tail = [upd_tail[reps[m], ROWS * e:ROWS * e + ROWS].astype(F32) for m in range(4)]
            tiles = [
                main[0],
                jnp.where(lane < 32, tail[0], main[1]),
                jnp.where(lane < 32, main[1], jnp.where(lane < 64, tail[1], main[2])),
                jnp.where(lane < 64, main[2], jnp.where(lane < 96, tail[2], main[3])),
                jnp.where(lane < 96, main[3], tail[3]),
            ]
            for k in range(5):
                cols = slice(640 * q + 128 * k, 640 * q + 128 * k + 128)
                m_new = 0.9 * mo[e, :, cols] + tiles[k]
                mo[e, :, cols] = m_new
                th[e, :, cols] = th[e, :, cols] - 0.7 * (tiles[k] + 0.9 * m_new)
        for c in write(q):
            c.start()
    for q in range(8):
        for c in write(q):
            c.wait()
    moved.wait()


def finish(upd, upd_tail, err, theta, momentum):
    vmem = pl.BlockSpec(memory_space=pltpu.VMEM)
    hbm = pl.BlockSpec(memory_space=pl.ANY)
    return pl.pallas_call(
        finish_kernel,
        out_shape=(
            jax.ShapeDtypeStruct(theta.shape, F32),
            jax.ShapeDtypeStruct(theta.shape, F32),
            jax.ShapeDtypeStruct(err.shape, BF16),
        ),
        in_specs=[vmem, vmem, vmem, hbm, hbm],
        out_specs=(hbm, hbm, hbm),
        scratch_shapes=[
            pltpu.VMEM((2, ROWS, 5120), F32),
            pltpu.VMEM((2, ROWS, 5120), F32),
            pltpu.SemaphoreType.DMA,
            pltpu.SemaphoreType.DMA((8,)),
            pltpu.SemaphoreType.DMA((8,)),
            pltpu.SemaphoreType.DMA((8,)),
            pltpu.SemaphoreType.DMA((8,)),
        ],
        compiler_params=pltpu.CompilerParams(vmem_limit_bytes=16 << 20),
        name="finish",
    )(upd, upd_tail, err, theta, momentum)


def shards(delta, error, theta, momentum, block_index, block_count):
    idx, count = block_index[0], block_count[0]
    live = jnp.arange(16, dtype=I32)[None, :] < count[:, None]
    idx = jnp.where(live, idx, -1)
    idx = jnp.pad(idx, ((0, 1), (0, 0)), constant_values=-1)
    own_idx = jnp.tile(idx, (1, R))
    flat_idx = jnp.broadcast_to(idx.reshape(1, SPAN), (8, SPAN))
    cos = jnp.asarray(cosine_parts())
    err = jnp.transpose(error[0], (0, 2, 1))
    upd, upd_tail, err_new = exchange(delta[0], err, cos, own_idx, flat_idx)
    theta_new, momentum_new, err_new = finish(upd, upd_tail, err_new, theta, momentum)
    return theta_new, momentum_new, jnp.transpose(err_new, (0, 2, 1))[None]


def solution(mesh):
    return jax.shard_map(
        shards,
        mesh=mesh,
        in_specs=(
            P("replica", None, "fsdp", None),
            P("replica", None, None, "fsdp"),
            P(None, "fsdp", None),
            P(None, "fsdp", None),
            P("replica", "fsdp", None),
            P("replica", "fsdp"),
        ),
        out_specs=(P(None, "fsdp", None), P(None, "fsdp", None), P("replica", None, None, "fsdp")),
        check_vma=False,
    )
```

time: 225 us -> 67 us (0.30); the launches traced: 221 us -> 66.7 us
  waiting for transfers between devices: 102 us -> 0 us
  Pallas kernels: 0 us -> 60 us
  local copies, waits for them, and re-layouts: 52.3 us -> 5.17 us
  starting transfers between devices: 22.2 us -> 0 us
  other arithmetic: 15.7 us -> 0.91 us
  matrix products: 14.7 us -> 0 us
  between operations: 14.1 us -> 0.68 us
    psum x1 -> x0, waiting for transfers between devices: 65.9 us -> none  [shards(): lax.psum(own_dense.astype(jnp.bfloat16), 'replica').astype(jnp.float32)]
    pallas_call x0 -> x2, Pallas kernels: none -> 60 us  [the longest x1 57.1 us: exchange(): pl.pallas_call(exchange_kernel, out_shape=(pltpu.VMEM((2, R, 4, ROWS, 128...]
    all_to_all x2 -> x0, waiting for transfers between devices: 36.1 us -> none  [the longest x1 20.5 us: shards(): lax.all_to_all(update_cols.astype(jnp.bfloat16), 'fsdp', split_axis=1, co...]
    all_to_all x2 -> x0, starting transfers between devices: 21.9 us -> none  [the longest x1 12 us: shards(): lax.all_to_all(delta[0], 'fsdp', split_axis=2, concat_axis=1, tiled=True)]
    convert_element_type x5 -> x0, local copies, waits for them, and re-layouts: 20 us -> none  [the longest x2 8.22 us: shards(): columns.astype(jnp.float32)]
    unnamed x13 -> x10, local copies, waits for them, and re-layouts: 23 us -> 4.99 us
    dot_general x5 -> x0, matrix products: 14.7 us -> none  [the longest x2 9.03 us: inverse_spans(): jnp.einsum('kt,kecf->ectf', cosines, shaped, precision=lax.Precision.HIGH...]
    sub x1 -> x0, other arithmetic: 4.73 us -> none  [shards(): theta_new = theta - outer_rate * (update + outer_momentum * momentum_new)]
  transfers between devices with their start and end apart: 3 -> 0, of which waited for: 3 -> 0; matrix products, arithmetic and copies ran while one was open for 10% -> 0% of each run, Pallas kernels for 0% -> 0%
where the time goes in v1:
time: 67 us; the launch traced here: 66.7 us
  Pallas kernels  60 us (90%)
  local copies, waits for them, and re-layouts  5.17 us (8%)
  other arithmetic  0.91 us (1%)
  between operations  0.68 us (1%)
    pallas_call x1, Pallas kernels, exchange(): pl.pallas_call(exchange_kernel, out_shape=(pltpu.VMEM((2, R, 4, ROWS, 128...  57.1 us
    unnamed x10, local copies, waits for them, and re-layouts  4.99 us
    pallas_call x1, Pallas kernels, finish(): pl.pallas_call(finish_kernel, out_shape=(jax.ShapeDtypeStruct(theta.shape...  2.83 us

profile of v1, /device:TPU:1, one launch (start us, length us, event | category | flops | bytes accessed | tf_op | source)
XLA Modules:
  0.0 66.7 jit_solution(5106175595603707003)
XLA Ops:
  0.6 0.0 copy-start
  0.6 0.9 %bitcast_select_fusion = s32[15,16]{1,0:T(8,128)S(1)} fusion(s32[1,15,16]{2,0,1:T(1,128)} %param.11, s32[15]{0:T(128)} %bitcast.12), kind=kLoop, calls=%fused_computation | loop fusion | flops 480 | bytes 1980 | tf_op jit(solution)/shard_map/jit(_where)/select_n | solution.py:584
  1.6 0.1 broadcast_in_dim.16
  1.7 0.1 tile.10.own_idx
  1.7 0.0 copy-start.2
  1.7 1.2 %copy-done.2 = bf16[1,2,48,5120]{3,2,1,0:T(8,128)(2,1)S(1)} copy-done((bf16[1,2,48,5120]{3,2,1,0:T(8,128)(2,1)S(1)}, bf16[1,2,48,5120]{3,2,1,0:T(8,128)(2,1)}, u32[]{:S(2)}) %copy-start.2) | copy-done | bytes 983064
  2.9 0.0 copy-start.3
  2.9 1.2 %copy-done.3 = bf16[1,2,1536,160]{2,3,1,0:T(8,128)(2,1)S(1)} copy-done((bf16[1,2,1536,160]{2,3,1,0:T(8,128)(2,1)S(1)}, bf16[1,2,1536,160]{2,3,1,0:T(8,128)(2,1)}, u32[]{:S(2)}) %copy-start.3) | copy-done | bytes 983064
  4.1 0.0 copy-start.4
  4.1 1.0 %copy-done.4 = bf16[4,256,256]{2,1,0:T(8,128)(2,1)S(1)} copy-done((bf16[4,256,256]{2,1,0:T(8,128)(2,1)S(1)}, bf16[4,256,256]{2,1,0:T(8,128)(2,1)}, u32[]{:S(2)}) %copy-start.4) | copy-done | bytes 524312
  5.2 57.1 %exchange.1 = (bf16[2,8,4,48,128]{4,3,2,1,0:T(8,128)(2,1)S(1)}, bf16[8,96,128]{2,1,0:T(8,128)(2,1)S(1)}, bf16[2,160,1536]{2,1,0:T(8,128)(2,1)S(1)}) custom-call(bf16[2,48,5120]{2,1,0:T(8,128)(2,1)S(1)} %bitcast.10, bf16[2,160,1536]{2,1,0:T(8,128)(2,1)S(1)} %bitcast.11, bf16[4,256,256]{2,1,0:T(8,128)(2,1)S(1)} %copy-done.4, s32[16,128]{1,0:T(8,128)S(1)} %tile.10.own_idx, ...), custom_call_target="tpu_custom_call" | custom-call | tf_op jit(solution)/shard_map/exchange/pallas_call | solution.py:454
  62.3 0.0 copy-done
  62.3 0.0 copy-start.1
  62.4 1.5 %copy-done.1 = f32[2,48,5120]{2,1,0:T(8,128)S(1)} copy-done((f32[2,48,5120]{2,1,0:T(8,128)S(1)}, f32[2,48,5120]{2,1,0:T(8,128)}, u32[]{:S(2)}) %copy-start.1) | copy-done | bytes 1966104
  63.9 2.8 %finish.1 = (f32[2,48,5120]{2,1,0:T(8,128)}, f32[2,48,5120]{2,1,0:T(8,128)}, bf16[2,160,1536]{2,1,0:T(8,128)(2,1)}) custom-call(bf16[2,8,4,48,128]{4,3,2,1,0:T(8,128)(2,1)S(1)} %get-tuple-element.9.upd, bf16[8,96,128]{2,1,0:T(8,128)(2,1)S(1)} %get-tuple-element.10.upd_tail, bf16[2,160,1536]{2,1,0:T(8,128)(2,1)S(1)} %get-tuple-element.11.err, ...), custom_call_target="tpu_custom_call" | custom-call | tf_op jit(solution)/shard_map/finish/pallas_call | solution.py:558
  (3 shorter events, 0.0 us)
Async XLA Ops:
  0.6 61.7 %copy-start = (f32[2,48,5120]{2,1,0:T(8,128)S(1)}, f32[2,48,5120]{2,1,0:T(8,128)}, u32[]{:S(2)}) copy-start(f32[2,48,5120]{2,1,0:T(8,128)} %theta.1) | copy-start | bytes 5898244
  1.7 1.2 %copy-start.2 = (bf16[1,2,48,5120]{3,2,1,0:T(8,128)(2,1)S(1)}, bf16[1,2,48,5120]{3,2,1,0:T(8,128)(2,1)}, u32[]{:S(2)}) copy-start(bf16[1,2,48,5120]{3,2,1,0:T(8,128)(2,1)} %param.7) | copy-start | bytes 2949124
  2.9 1.2 %copy-start.3 = (bf16[1,2,1536,160]{2,3,1,0:T(8,128)(2,1)S(1)}, bf16[1,2,1536,160]{2,3,1,0:T(8,128)(2,1)}, u32[]{:S(2)}) copy-start(bf16[1,2,1536,160]{2,3,1,0:T(8,128)(2,1)} %param.8) | copy-start | bytes 2949124
  4.1 1.0 %copy-start.4 = (bf16[4,256,256]{2,1,0:T(8,128)(2,1)S(1)}, bf16[4,256,256]{2,1,0:T(8,128)(2,1)}, u32[]{:S(2)}) copy-start(bf16[4,256,256]{2,1,0:T(8,128)(2,1)} %constant.4.clone.cos) | copy-start | bytes 1572868
  62.3 1.5 %copy-start.1 = (f32[2,48,5120]{2,1,0:T(8,128)S(1)}, f32[2,48,5120]{2,1,0:T(8,128)}, u32[]{:S(2)}) copy-start(f32[2,48,5120]{2,1,0:T(8,128)} %momentum.1) | copy-start | bytes 5898244

commit v2 on v1

v2 whole, which is shorter than its diff:
```python
import functools

import jax
import jax.numpy as jnp
import numpy as np
from jax import lax
from jax.experimental import pallas as pl
from jax.experimental.pallas import tpu as pltpu
from jax.sharding import PartitionSpec as P

SPAN = 256
N = 32
R = 8
ROWS = 48
MESH = pl.DeviceIdType.MESH
F32 = jnp.float32
BF16 = jnp.bfloat16
I32 = jnp.int32


def cosine_table():
    k = np.arange(SPAN, dtype=np.float64)[:, None]
    t = np.arange(SPAN, dtype=np.float64)[None, :]
    m = np.cos(np.pi * (2.0 * t + 1.0) * k / (2.0 * SPAN))
    return (m * np.where(k == 0, np.sqrt(1.0 / SPAN), np.sqrt(2.0 / SPAN))).astype(np.float32)


def div(a, b):
    return lax.div(a, jnp.int32(b))


def rem(a, b):
    return lax.rem(a, jnp.int32(b))


def turn_of(f):
    y, z = div(f, 8), rem(f, 8)
    return 2 * rem(y + z, 4) + div(z, 4)


PIECES = (
    [(48 * n, 0, 48) for n in range(5)] + [(240, 0, 16)],
    [(0, 16, 32)] + [(32 + 48 * n, 0, 48) for n in range(4)] + [(224, 0, 32)],
    [(0, 32, 16)] + [(16 + 48 * n, 0, 48) for n in range(5)],
)


def dot_nt(a, b):
    return lax.dot_general(a, b, (((1,), (1,)), ((), ())), preferred_element_type=F32)


def dot_tn(a, b):
    return lax.dot_general(a, b, (((0,), (0,)), ((), ())), preferred_element_type=F32)


def dot(a, b):
    return jnp.dot(a, b, preferred_element_type=F32)


def lanes(shape):
    return lax.broadcasted_iota(I32, shape, len(shape) - 1)


def exchange_kernel(
    delta, err, cos, idx, count, theta, momentum,
    upd, upd_tail, err_out, theta_v, momentum_v,
    d_v, e_v, table, cos_v, idx_v, count_s, lists, own_idx, send, send_t, recv, recv_t, x_t, low, basis,
    from_err, idx_all, merged, kept, kept_in, u_out, u_tail, u_msg, u_recv,
    load_sem, a2a_s, a2a_r, idx_s, idx_r, kept_s, kept_r, upd_s, upd_r, fwd_s, fwd_r,
):
    r = lax.axis_index("replica")
    f = lax.axis_index("fsdp")
    y, z = div(f, 8), rem(f, 8)
    fm = rem(f, 4)
    turn = turn_of(f)
    mine_first = rem(r - turn + R, R)
    has_second = mine_first < 4
    block_of = (mine_first, jnp.where(mine_first < 4, mine_first + 8, mine_first), mine_first,
                rem(mine_first, 4) + 8)
    has_block = (mine_first < 6, (mine_first < 4) | (mine_first >= 6), None, has_second)

    loads = [
        pltpu.make_async_copy(delta.at[0], d_v.at[0], load_sem.at[0]),
        pltpu.make_async_copy(delta.at[1], d_v.at[1], load_sem.at[1]),
        pltpu.make_async_copy(cos, table, load_sem.at[2]),
        pltpu.make_async_copy(err, e_v, load_sem.at[3]),
        pltpu.make_async_copy(idx, idx_v, load_sem.at[4]),
        pltpu.make_async_copy(count, count_s, load_sem.at[5]),
        pltpu.make_async_copy(theta, theta_v, load_sem.at[6]),
        pltpu.make_async_copy(momentum, momentum_v, load_sem.at[7]),
    ]
    for c in loads[:6]:
        c.start()

    bar = pltpu.get_barrier_semaphore()

    def greet_row(o, _):
        pl.semaphore_signal(bar, inc=1, device_id=(r, rem(f + o, N)), device_id_type=MESH)
        return 0

    def greet_col(o, _):
        pl.semaphore_signal(bar, inc=1, device_id=(rem(r + o, R), f), device_id_type=MESH)
        return 0

    lax.fori_loop(1, N, greet_row, 0)
    lax.fori_loop(1, R, greet_col, 0)

    lane16 = lanes((16, 128))

    def pack_main(e):
        def body(q, _):
            for i in range(3):
                rows = pl.ds(16 * i, 16)
                t = [
                    d_v[e, rows, pl.ds(pl.multiple_of(640 * q + 128 * k, 128), 128)]
                    for k in range(5)
                ]
                send[e, 4 * q, rows] = t[0]
                send[e, 4 * q + 1, rows] = jnp.where(lane16 >= 32, t[1], t[2])
                send[e, 4 * q + 2, rows] = jnp.where(lane16 >= 64, t[2], t[3])
                send[e, 4 * q + 3, rows] = jnp.where(lane16 >= 96, t[3], t[4])
            return 0

        lax.fori_loop(0, 8, body, 0)

    def pack_tail():
        def body(q, _):
            zs = []
            for g in range(6):
                e, i = g // 3, g % 3
                t = [
                    d_v[e, 16 * i:16 * i + 16, pl.ds(pl.multiple_of(640 * q + 128 * k, 128), 128)]
                    for k in range(1, 5)
                ]
                v = jnp.where(
                    lane16 < 32, t[0], jnp.where(lane16 < 64, t[1], jnp.where(lane16 < 96, t[2], t[3]))
                )
                zs.append(v.astype(F32))
            for m in range(4):
                w = [None, None]
                for g in range(6):
                    k = g % 4
                    s = (32 * (k - m)) % 128
                    v = pltpu.roll(zs[g], s, 1) if s else zs[g]
                    p = w[g // 4]
                    w[g // 4] = v if p is None else jnp.where(lane16 < 32 * k, p, v)
                send_t[4 * q + m, 0:16] = w[0].astype(BF16)
                send_t[4 * q + m, 16:32] = w[1].astype(BF16)
            return 0

        lax.fori_loop(0, 8, body, 0)

    def offsets(half, dy):
        turns = ((1, -1, 2, -2), (3, -3, 4, 0))[half]
        return [(dy, dz) for dz in turns if dy or dz]

    def group_ref(j):
        n = len(offsets(j % 2, j % 8 // 2))
        return send.at[j // 8, pl.ds(0, n)] if j < 16 else send_t.at[pl.ds(0, n)]

    def group_start(j):
        p = j // 8
        for dy, dz in offsets(j % 2, j % 8 // 2):
            d = 8 * rem(y + dy, 4) + rem(z + dz + 8, 8)
            if p < 2:
                src, dst = send.at[p, d], recv.at[p, pl.ds(pl.multiple_of(ROWS * f, 16), ROWS)]
            else:
                src, dst = send_t.at[d], recv_t.at[f]
            pltpu.make_async_remote_copy(
                src_ref=src, dst_ref=dst, send_sem=a2a_s.at[j], recv_sem=a2a_r.at[p],
                device_id=(r, d), device_id_type=MESH,
            ).start()

    def group_wait(j):
        pltpu.make_async_copy(group_ref(j), group_ref(j), a2a_s.at[j]).wait()

    started = [0]

    def pump(upto):
        for j in range(started[0], upto):
            group_start(j)
        started[0] = max(started[0], upto)

    loads[0].wait()
    pack_main(0)
    pl.semaphore_wait(bar, N - 1 + R - 1)
    pump(8)
    loads[1].wait()
    pack_main(1)
    for c in loads[6:]:
        c.start()
    pump(16)
    pack_tail()
    for e in range(2):
        recv[e, pl.ds(pl.multiple_of(ROWS * f, 16), ROWS)] = send[e, f]
    recv_t[f] = send_t[f]

    loads[4].wait()
    loads[5].wait()
    lists[...] = jnp.full((16, 128), -1.0, F32)
    for g in range(15):
        named = jnp.where(lanes((1, 16)) < count_s[0, g], idx_v[g], -1)
        lists[g:g + 1, 0:16] = named.astype(F32)
    held = lists[...].astype(BF16)
    into, outof = lax.broadcasted_iota(I32, (128, 128), 0), lanes((128, 128))
    spread = jnp.where((into < 16) & (rem(outof, 16) == into), 1.0, 0.0).astype(BF16)
    own_idx[...] = dot(held, spread)

    idx_all[r] = own_idx[...]
    for o in range(1, R):
        pltpu.make_async_remote_copy(
            src_ref=own_idx, dst_ref=idx_all.at[r],
            send_sem=idx_s, recv_sem=idx_r, device_id=(rem(r + o, R), f), device_id_type=MESH,
        ).start()

    loads[2].wait()
    for way, full in enumerate((table[...], jnp.transpose(table[...]))):
        high = full.astype(BF16)
        cos_v[2 * way] = high
        cos_v[2 * way + 1] = (full - high.astype(F32)).astype(BF16)
    slot, group = lax.broadcasted_iota(I32, (SPAN, 16), 0), lanes((SPAN, 16))
    mine = dot(jnp.where(div(slot, 16) == group, 1.0, 0.0).astype(BF16), held)
    slot, lane = lax.broadcasted_iota(I32, (SPAN, 128), 0), lanes((SPAN, 128))
    mine = jnp.where(rem(slot, 16) == lane, mine, 0.0).astype(BF16)
    mine = dot(mine, jnp.ones((128, SPAN), BF16))
    pick = jnp.where(mine == lanes((SPAN, SPAN)).astype(F32), 1.0, 0.0).astype(BF16)
    for part in range(2):
        rows = dot(pick, cos_v[part]).astype(BF16)
        for g in range(15):
            low[32 * g + 16 * part:32 * g + 16 * part + 16] = rows[16 * g:16 * g + 16]

    part = idx_all.at[pl.ds(0, R - 1)]
    pltpu.make_async_copy(part, part, idx_r).wait()
    lists_all = idx_all[0]
    for p in range(1, R):
        lists_all = jnp.where(lane16 < 16 * p, lists_all, idx_all[p])
    merged[...] = lists_all
    kk = lax.broadcasted_iota(I32, (SPAN, 128), 0).astype(F32)
    first_a, first_b = div(5 * block_of[0], 4), div(5 * block_of[1], 4)
    first_a = jnp.minimum(first_a, 13)
    tails = [b + 1 + div(b, 4) for b in (mine_first, rem(mine_first, 4) + 8)]
    for s, g in enumerate((first_a, first_a + 1, first_b, first_b + 1, tails[0], tails[1])):
        hot = jnp.where(kk == merged[pl.ds(g, 1), :], 1.0, 0.0).astype(BF16)
        basis[s, :, 0:128] = dot(cos_v[2], hot).astype(BF16)
        basis[s, :, 128:256] = dot(cos_v[3], hot).astype(BF16)

    loads[3].wait()

    place16 = rem(lane16 - 32 * fm + 128, 128)
    place128 = rem(lanes((128, 128)) - 32 * fm + 128, 128)

    def turned(e, c):
        return jnp.concatenate(
            [
                e_v[e, pl.ds(pl.multiple_of(32 * rem(i - fm + 4, 4), 32), 32), SPAN * c:SPAN * c + SPAN]
                for i in range(4)
            ],
            axis=0,
        )

    def err_columns(tb):
        return jnp.concatenate(
            [
                e_v[(4 * tb + j) // 6, 128:160, SPAN * ((4 * tb + j) % 6):SPAN * ((4 * tb + j) % 6) + SPAN]
                for j in range(4)
            ],
            axis=0,
        )

    def main_rows(b):
        ga = (5 * b) // 4
        return low[32 * ga:32 * ga + 64]

    def tail_rows(tb):
        base = 32 * (5 * tb + 1)
        return low[base:base + 128]

    def main_select(b, o):
        pa, pb = o[0:16] + o[16:32], o[32:48] + o[48:64]
        return jnp.where(place16 < 128 - 32 * (b % 4), pa, pb)

    def tail_select(o):
        p = o[0:16] + o[16:32]
        for j in range(1, 4):
            p = jnp.where(lane16 < 32 * j, p, o[32 * j:32 * j + 16] + o[32 * j + 16:32 * j + 32])
        return p

    for b in range(12):
        from_err[b] = 0.95 * main_select(b, dot_nt(main_rows(b), turned(b // 6, b % 6)))
    for tb in range(3):
        from_err[12 + tb] = 0.95 * tail_select(dot_nt(tail_rows(tb), err_columns(tb)))

    def take_delta(p):
        part = recv.at[p, pl.ds(0, (N - 1) * ROWS)] if p < 2 else recv_t.at[pl.ds(0, N - 1)]
        pltpu.make_async_copy(part, part, a2a_r.at[p]).wait()

    def pick_main(e):
        take_delta(e)
        for c in range(6):
            b = 6 * e + c
            x = recv[e, SPAN * c:SPAN * c + SPAN]
            kept[b] = (main_select(b, dot(main_rows(b), x)) + from_err[b]).astype(BF16)

    def pick_tail():
        take_delta(2)
        for tb in range(3):
            for t16 in range(16):
                v = None
                for j in range(4):
                    b = 4 * tb + j
                    e, row = b // 6, SPAN * (b % 6) + 16 * t16
                    s, g = row // ROWS, 3 * e + (row % ROWS) // 16
                    w = recv_t[s, 16 * (g // 4):16 * (g // 4) + 16].astype(F32)
                    sh = (32 * (j - g)) % 128
                    w = pltpu.roll(w, sh, 1) if sh else w
                    v = w if v is None else jnp.where(lane16 < 32 * j, v, w)
                x_t[tb, 16 * t16:16 * t16 + 16] = v.astype(BF16)
            kept[12 + tb] = (tail_select(dot(tail_rows(tb), x_t[tb])) + from_err[12 + tb]).astype(BF16)

    def tile_of(slot, b8):
        if slot == 0:
            return jnp.minimum(b8, 5)
        if slot == 1:
            return jnp.where(b8 < 4, b8 + 8, jnp.maximum(b8, 6))
        return 12 + div(b8, 4) if slot == 2 else 14

    def send_kept(slot):
        rows = pl.ds(pl.multiple_of(16 * r, 16), 16)
        for o in range(1, R):
            pltpu.make_async_remote_copy(
                src_ref=kept.at[tile_of(slot, rem(mine_first + o, R))], dst_ref=kept_in.at[slot, rows],
                send_sem=kept_s.at[slot], recv_sem=kept_r.at[slot],
                device_id=(rem(r + o, R), f), device_id_type=MESH,
            ).start()
        pltpu.make_async_copy(
            kept.at[tile_of(slot, mine_first)], kept_in.at[slot, rows], kept_r.at[slot]
        ).start()

    def restore_main(e):
        for c in range(6):
            b = 6 * e + c
            k, zero = kept[b], jnp.zeros((16, 128), BF16)
            first = place16 < 128 - 32 * (b % 4)
            ka, kb = jnp.where(first, k, zero), jnp.where(first, zero, k)
            back = dot_tn(jnp.concatenate([ka, ka, kb, kb], axis=0), main_rows(b))
            x = recv[e, SPAN * c:SPAN * c + SPAN].astype(F32)
            en = (0.95 * turned(e, c).astype(F32) + jnp.transpose(x) - back).astype(BF16)
            for i in range(4):
                err_out[
                    e, pl.ds(pl.multiple_of(32 * rem(i - fm + 4, 4), 32), 32), SPAN * c:SPAN * c + SPAN
                ] = en[32 * i:32 * i + 32]

    def restore_tail():
        for tb in range(3):
            k, zero = kept[12 + tb], jnp.zeros((16, 128), BF16)
            ks = []
            for j in range(4):
                kj = jnp.where((lane16 >= 32 * j) & (lane16 < 32 * j + 32), k, zero)
                ks += [kj, kj]
            back = dot_tn(jnp.concatenate(ks, axis=0), tail_rows(tb))
            en = 0.95 * err_columns(tb).astype(F32) + jnp.transpose(x_t[tb].astype(F32)) - back
            en = en.astype(BF16)
            for j in range(4):
                e, c = (4 * tb + j) // 6, (4 * tb + j) % 6
                err_out[e, 128:160, SPAN * c:SPAN * c + SPAN] = en[32 * j:32 * j + 32]

    def when(flag, body):
        if flag is None:
            body()
        else:
            pl.when(flag)(body)

    def upd_move(s, v, n, what):
        b = block_of[s]
        e, c = div(b, 6), rem(b, 6)
        at, to, rows = PIECES[v][n]
        d = 16 * div(c, 3) + 5 * v + n
        if s < 2:
            src, dst = u_out.at[s, pl.ds(at, rows)], upd.at[s, r, y, pl.ds(to, rows)]
        else:
            src, dst = u_msg.at[s - 2, n], u_recv.at[1 if to else 0, e, y]
        arrived = upd_r.at[min(s, 2)]

        @pl.when(d != f)
        def _():
            m = pltpu.make_async_remote_copy(
                src_ref=src, dst_ref=dst, send_sem=upd_s.at[s, n], recv_sem=arrived,
                device_id=(r, d), device_id_type=MESH,
            )
            m.start() if what == "start" else m.wait_send()

        if what == "start":
            @pl.when(d == f)
            def _():
                pltpu.make_async_copy(src, dst, arrived).start()

    def upd_all(s, what):
        for v in range(3):
            @pl.when(rem(rem(block_of[s], 6), 3) == v)
            def _():
                for n in range(6):
                    upd_move(s, v, n, what)

    def take_kept(s):
        pltpu.make_async_copy(kept_in.at[s], kept_in.at[s], kept_r.at[s]).wait()
        return kept_in[s]

    def average_main(s):
        k = take_kept(s)
        zero = jnp.zeros_like(k)
        first = place128 < 128 - 32 * rem(block_of[s], 4)
        ka = jnp.where(first, k, zero)
        kb = jnp.where(first, zero, k)
        u = dot(basis[2 * s], jnp.concatenate([ka, ka], axis=0))
        u = u + dot(basis[2 * s + 1], jnp.concatenate([kb, kb], axis=0))
        u_out[s] = (u * 0.125).astype(BF16)
        when(has_block[s], functools.partial(upd_all, s, "start"))

    def average_tail():
        into, outof = lax.broadcasted_iota(I32, (128, 128), 0), lanes((128, 128))
        same = (div(into, 32) == rem(mine_first, 4)) & (rem(into, 32) == rem(outof, 32))
        same = jnp.where(same, 1.0, 0.0).astype(BF16)
        ks = [dot(take_kept(s), same).astype(BF16) for s in (2, 3)]
        for s in (2, 3):
            k = ks[s - 2]
            u_tail[s - 2] = dot(basis[2 + s], jnp.concatenate([k, k], axis=0)) * 0.125
        for s in (2, 3):
            for v in range(3):
                @pl.when(rem(rem(block_of[s], 6), 3) == v)
                def _():
                    for n, (at, to, rows) in enumerate(PIECES[v]):
                        w = None
                        for i in range(rows // 16):
                            x = u_tail[s - 2, at + 16 * i:at + 16 * i + 16]
                            w = x if w is None else jnp.where(lane16 < to * 2 + 32 * i, w, x)
                        u_msg[s - 2, n] = w.astype(BF16)
            when(has_block[s], functools.partial(upd_all, s, "start"))

    chunk = [div(3 * f + i, 16) for i in range(3)]

    def wait_upd(p):
        def some(part):
            pltpu.make_async_copy(part, part, upd_r.at[p]).wait()

        if p < 2:
            some(upd.at[p, 0])
            return

        @pl.when(chunk[0] == chunk[2])
        def _():
            some(u_recv.at[0])

        @pl.when(chunk[0] != chunk[2])
        def _():
            some(u_recv)

    def fwd_copy(p, other):
        ref = upd.at[p, r] if p < 2 else upd_tail.at[r]
        return pltpu.make_async_remote_copy(
            src_ref=ref, dst_ref=ref, send_sem=fwd_s.at[p], recv_sem=fwd_r.at[p],
            device_id=(other, f), device_id_type=MESH,
        )

    def forward(p):
        wait_upd(p)
        if p == 2:
            for e in range(2):
                for i in range(3):
                    whole = jnp.zeros((16, 128), F32)
                    behind = div(rem(r - 6 * e - chunk[i] + 2 * R, R), 2)
                    for yy in range(4):
                        m = rem(behind - yy + 4, 4)
                        v = u_recv[chunk[i] - chunk[0], e, yy].astype(F32)
                        v = pltpu.roll(v, rem(32 * (m - i) + 128, 128), 1)
                        whole = jnp.where(div(lane16, 32) == m, v, whole)
                    upd_tail[r, ROWS * e + 16 * i:ROWS * e + 16 * i + 16] = whole.astype(BF16)
        for o in range(1, R):
            fwd_copy(p, rem(r + o, R)).start()

    pick_main(0)
    send_kept(0)
    restore_main(0)
    pump(20)
    average_main(0)
    pump(24)
    pick_main(1)
    send_kept(1)
    forward(0)
    restore_main(1)
    average_main(1)
    pick_tail()
    send_kept(2)
    send_kept(3)
    average_tail()
    forward(1)
    restore_tail()
    forward(2)

    for p in range(3):
        part = upd.at[p, pl.ds(0, R - 1)] if p < 2 else upd_tail.at[pl.ds(0, R - 1)]
        pltpu.make_async_copy(part, part, fwd_r.at[p]).wait()
        pltpu.make_async_copy(part, part, fwd_s.at[p]).wait()

    for j in range(24):
        group_wait(j)
    for c in loads[6:]:
        c.wait()

    part = idx_all.at[pl.ds(0, R - 1)]
    pltpu.make_async_copy(part, part, idx_s).wait()
    for s in range(4):
        pltpu.make_async_copy(
            kept_in.at[s, pl.ds(0, 16 * (R - 1))], kept_in.at[s, pl.ds(0, 16 * (R - 1))], kept_s.at[s]
        ).wait()
    for s in range(4):
        when(has_block[s], functools.partial(upd_all, s, "wait"))


def exchange(delta, err, cos, idx, count, theta, momentum):
    vmem = pl.BlockSpec(memory_space=pltpu.VMEM)
    hbm = pl.BlockSpec(memory_space=pltpu.HBM)
    args = (delta, err, cos, idx, count, theta, momentum)
    args = [pltpu.with_memory_space_constraint(a, pltpu.HBM) for a in args]
    return pl.pallas_call(
        exchange_kernel,
        out_shape=(
            pltpu.VMEM((2, R, 4, ROWS, 128), BF16),
            pltpu.VMEM((R, 2 * ROWS, 128), BF16),
            pltpu.VMEM((2, 160, 1536), BF16),
            pltpu.VMEM(theta.shape, F32),
            pltpu.VMEM(theta.shape, F32),
        ),
        in_specs=[hbm] * 7,
        out_specs=(vmem,) * 5,
        scratch_shapes=[
            pltpu.VMEM((2, ROWS, 5120), BF16),
            pltpu.VMEM((2, 160, 1536), BF16),
            pltpu.VMEM((SPAN, SPAN), F32),
            pltpu.VMEM((4, SPAN, SPAN), BF16),
            pltpu.VMEM((15, 1, 16), I32),
            pltpu.SMEM((1, 15), I32),
            pltpu.VMEM((16, 128), F32),
            pltpu.VMEM((16, 128), F32),
            pltpu.VMEM((2, N, ROWS, 128), BF16),
            pltpu.VMEM((N, 32, 128), BF16),
            pltpu.VMEM((2, N * ROWS, 128), BF16),
            pltpu.VMEM((N, 32, 128), BF16),
            pltpu.VMEM((3, SPAN, 128), BF16),
            pltpu.VMEM((15 * 32, SPAN), BF16),
            pltpu.VMEM((6, SPAN, SPAN), BF16),
            pltpu.VMEM((15, 16, 128), F32),
            pltpu.VMEM((R, 16, 128), F32),
            pltpu.VMEM((16, 128), F32),
            pltpu.VMEM((15, 16, 128), BF16),
            pltpu.VMEM((4, 128, 128), BF16),
            pltpu.VMEM((2, SPAN, 128), BF16),
            pltpu.VMEM((2, SPAN, 128), F32),
            pltpu.VMEM((2, 6, 16, 128), BF16),
            pltpu.VMEM((2, 2, 4, 16, 128), BF16),
            pltpu.SemaphoreType.DMA((8,)),
            pltpu.SemaphoreType.DMA((24,)),
            pltpu.SemaphoreType.DMA((3,)),
            pltpu.SemaphoreType.DMA,
            pltpu.SemaphoreType.DMA,
            pltpu.SemaphoreType.DMA((4,)),
            pltpu.SemaphoreType.DMA((4,)),
            pltpu.SemaphoreType.DMA((4, 6)),
            pltpu.SemaphoreType.DMA((3,)),
            pltpu.SemaphoreType.DMA((3,)),
            pltpu.SemaphoreType.DMA((3,)),
        ],
        compiler_params=pltpu.CompilerParams(
            collective_id=0, has_side_effects=True, vmem_limit_bytes=32 << 20
        ),
        name="exchange",
    )(*args)


def finish_kernel(
    upd, upd_tail, err, theta, momentum,
    theta_out, momentum_out, err_out,
    th, mo, err_sem, th_sem, mo_sem,
):
    moved = pltpu.make_async_copy(err, err_out, err_sem)
    moved.start()

    def write(q):
        cols = pl.ds(640 * q, 640)
        return (
            pltpu.make_async_copy(th.at[:, :, cols], theta_out.at[:, :, cols], th_sem.at[q]),
            pltpu.make_async_copy(mo.at[:, :, cols], momentum_out.at[:, :, cols], mo_sem.at[q]),
        )

    f = lax.axis_index("fsdp")
    lane = lanes((16, 128))
    for q in range(8):
        y, core = q // 2, q % 2
        for e in range(2):
            for i in range(3):
                rows = slice(16 * i, 16 * i + 16)
                shift = 6 * e + div(3 * f + i, 16) + core
                reps = [rem(shift + 2 * ((y + m) % 4), R) for m in range(4)]
                main = [upd[e, reps[m], y, rows].astype(F32) for m in range(4)]
                tail = [
                    upd_tail[reps[m], ROWS * e + 16 * i:ROWS * e + 16 * i + 16].astype(F32)
                    for m in range(4)
                ]
                tiles = [
                    main[0],
                    jnp.where(lane < 32, tail[0], main[1]),
                    jnp.where(lane < 32, main[1], jnp.where(lane < 64, tail[1], main[2])),
                    jnp.where(lane < 64, main[2], jnp.where(lane < 96, tail[2], main[3])),
                    jnp.where(lane < 96, main[3], tail[3]),
                ]
                for k in range(5):
                    cols = slice(640 * q + 128 * k, 640 * q + 128 * k + 128)
                    m_new = 0.9 * momentum[e, rows, cols] + tiles[k]
                    mo[e, rows, cols] = m_new
                    th[e, rows, cols] = theta[e, rows, cols] - 0.7 * (tiles[k] + 0.9 * m_new)
        for c in write(q):
            c.start()
    for q in range(8):
        for c in write(q):
            c.wait()
    moved.wait()


def finish(*args):
    vmem = pl.BlockSpec(memory_space=pltpu.VMEM)
    hbm = pl.BlockSpec(memory_space=pltpu.HBM)
    upd, upd_tail, err, theta, momentum = args
    args = [pltpu.with_memory_space_constraint(a, pltpu.VMEM) for a in args]
    return pl.pallas_call(
        finish_kernel,
        out_shape=(
            jax.ShapeDtypeStruct(theta.shape, F32),
            jax.ShapeDtypeStruct(theta.shape, F32),
            jax.ShapeDtypeStruct(err.shape, BF16),
        ),
        in_specs=[vmem] * 5,
        out_specs=(hbm, hbm, hbm),
        scratch_shapes=[
            pltpu.VMEM((2, ROWS, 5120), F32),
            pltpu.VMEM((2, ROWS, 5120), F32),
            pltpu.SemaphoreType.DMA,
            pltpu.SemaphoreType.DMA((8,)),
            pltpu.SemaphoreType.DMA((8,)),
        ],
        compiler_params=pltpu.CompilerParams(vmem_limit_bytes=16 << 20),
        name="finish",
    )(*args)


def shards(delta, error, theta, momentum, block_index, block_count):
    cos = jnp.asarray(cosine_table())
    err = jnp.transpose(error[0], (0, 2, 1))
    idx = block_index.reshape(15, 1, 16)
    made = exchange(delta[0], err, cos, idx, block_count, theta, momentum)
    theta_new, momentum_new, err_new = finish(*made)
    return theta_new, momentum_new, jnp.transpose(err_new, (0, 2, 1))[None]


def solution(mesh):
    return jax.shard_map(
        shards,
        mesh=mesh,
        in_specs=(
            P("replica", None, "fsdp", None),
            P("replica", None, None, "fsdp"),
            P(None, "fsdp", None),
            P(None, "fsdp", None),
            P("replica", "fsdp", None),
            P("replica", "fsdp"),
        ),
        out_specs=(P(None, "fsdp", None), P(None, "fsdp", None), P("replica", None, None, "fsdp")),
        check_vma=False,
    )
```

time: 67 us -> 57.5 us (0.86)
  local copies, waits for them, and re-layouts: 5.17 us -> 0 us
  Pallas kernels: 60 us -> 56.7 us
  other arithmetic: 0.91 us -> 0 us
    unnamed x10 -> x0, local copies, waits for them, and re-layouts: 4.99 us -> none
    pallas_call x1, Pallas kernels: 57.1 us -> 54.2 us  [exchange(): pl.pallas_call(exchange_kernel, out_shape=(pltpu.VMEM((2, R, 4, ROWS, 128...]
    select_n x1 -> x0, other arithmetic: 0.91 us -> none  [shards(): idx = jnp.where(live, idx, -1)]
where the time goes in v2:
time: 57.5 us; the launch traced here: 57.4 us
  Pallas kernels  56.7 us (99%)
  between operations  0.64 us (1%)
    pallas_call x1, Pallas kernels, exchange(): pl.pallas_call(exchange_kernel, out_shape=(pltpu.VMEM((2, R, 4, ROWS, 128...  54.2 us
    pallas_call x1, Pallas kernels, finish(): pl.pallas_call(finish_kernel, out_shape=(jax.ShapeDtypeStruct(theta.shape...  2.5 us

profile of v2, /device:TPU:1, one launch (start us, length us, event | category | flops | bytes accessed | tf_op | source)
XLA Modules:
  0.0 57.4 jit_solution(5576169666876741073)
XLA Ops:
  0.6 54.2 %exchange.1 = (bf16[2,8,4,48,128]{4,3,2,1,0:T(8,128)(2,1)S(1)}, bf16[8,96,128]{2,1,0:T(8,128)(2,1)S(1)}, bf16[2,160,1536]{2,1,0:T(8,128)(2,1)S(1)}, f32[2,48,5120]{2,1,0:T(8,128)S(1)}, f32[2,48,5120]{2,1,0:T(8,128)S(1)}) custom-call(bf16[2,48,5120]{2,1,0:T(8,128)(2,1)} %bitcast.8, bf16[2,160,1536]{2,1,0:T(8,128)(2,1)} %bitcast.9, ...), custom_call_target="tpu_custom_call" | custom-call | tf_op jit(solution)/shard_map/exchange/pallas_call | solution.py:524
  54.9 2.5 %finish.1 = (f32[2,48,5120]{2,1,0:T(8,128)}, f32[2,48,5120]{2,1,0:T(8,128)}, bf16[2,160,1536]{2,1,0:T(8,128)(2,1)}) custom-call(bf16[2,8,4,48,128]{4,3,2,1,0:T(8,128)(2,1)S(1)} %get-tuple-element.11.upd, bf16[8,96,128]{2,1,0:T(8,128)(2,1)S(1)} %get-tuple-element.12.upd_tail, bf16[2,160,1536]{2,1,0:T(8,128)(2,1)S(1)} %get-tuple-element.13.err, ...), custom_call_target="tpu_custom_call" | custom-call | tf_op jit(solution)/shard_map/finish/pallas_call | solution.py:633

commit v3 on v2

--- a/solution.py
+++ b/solution.py
@@ -63,10 +63,11 @@
 
 def exchange_kernel(
     delta, err, cos, idx, count, theta, momentum,
-    upd, upd_tail, err_out, theta_v, momentum_v,
+    upd, upd_tail, last_tail, err_out, theta_v, momentum_v,
     d_v, e_v, table, cos_v, idx_v, count_s, lists, own_idx, send, send_t, recv, recv_t, x_t, low, basis,
     from_err, idx_all, merged, kept, kept_in, u_out, u_tail, u_msg, u_recv,
-    load_sem, a2a_s, a2a_r, idx_s, idx_r, kept_s, kept_r, upd_s, upd_r, fwd_s, fwd_r,
+    kept_last, basis_last, u_last, last_msg, last_recv,
+    load_sem, a2a_s, a2a_r, idx_s, idx_r, kept_s, kept_r, upd_s, upd_r, fwd_s, fwd_r, last_s, last_r,
 ):
     r = lax.axis_index("replica")
     f = lax.axis_index("fsdp")
@@ -74,10 +75,8 @@
     fm = rem(f, 4)
     turn = turn_of(f)
     mine_first = rem(r - turn + R, R)
-    has_second = mine_first < 4
-    block_of = (mine_first, jnp.where(mine_first < 4, mine_first + 8, mine_first), mine_first,
-                rem(mine_first, 4) + 8)
-    has_block = (mine_first < 6, (mine_first < 4) | (mine_first >= 6), None, has_second)
+    block_of = (mine_first, jnp.where(mine_first < 4, mine_first + 8, mine_first))
+    has_block = (mine_first < 6, (mine_first < 4) | (mine_first >= 6))
 
     loads = [
         pltpu.make_async_copy(delta.at[0], d_v.at[0], load_sem.at[0]),
@@ -89,21 +88,19 @@
         pltpu.make_async_copy(theta, theta_v, load_sem.at[6]),
         pltpu.make_async_copy(momentum, momentum_v, load_sem.at[7]),
     ]
-    for c in loads[:6]:
+    loads[0].start()
+
+    bar = pltpu.get_barrier_semaphore()
+
+    for dy in (2, 1, 3, 0):
+        for dz in (4, 3, -3, 2, -2, 1, -1, 0):
+            if dy or dz:
+                d = 8 * rem(y + dy, 4) + rem(z + dz + 8, 8)
+                pl.semaphore_signal(bar, inc=1, device_id=(r, d), device_id_type=MESH)
+    for o in (4, 3, 5, 2, 6, 1, 7):
+        pl.semaphore_signal(bar, inc=1, device_id=(rem(r + o, R), f), device_id_type=MESH)
+    for c in loads[1:6]:
         c.start()
-
-    bar = pltpu.get_barrier_semaphore()
-
-    def greet_row(o, _):
-        pl.semaphore_signal(bar, inc=1, device_id=(r, rem(f + o, N)), device_id_type=MESH)
-        return 0
-
-    def greet_col(o, _):
-        pl.semaphore_signal(bar, inc=1, device_id=(rem(r + o, R), f), device_id_type=MESH)
-        return 0
-
-    lax.fori_loop(1, N, greet_row, 0)
-    lax.fori_loop(1, R, greet_col, 0)
 
     lane16 = lanes((16, 128))
 
@@ -123,11 +120,10 @@
 
         lax.fori_loop(0, 8, body, 0)
 
-    def pack_tail():
+    def pack_tail(e):
         def body(q, _):
             zs = []
-            for g in range(6):
-                e, i = g // 3, g % 3
+            for i in range(3):
                 t = [
                     d_v[e, 16 * i:16 * i + 16, pl.ds(pl.multiple_of(640 * q + 128 * k, 128), 128)]
                     for k in range(1, 5)
@@ -137,26 +133,23 @@
                 )
                 zs.append(v.astype(F32))
             for m in range(4):
-                w = [None, None]
-                for g in range(6):
-                    k = g % 4
-                    s = (32 * (k - m)) % 128
-                    v = pltpu.roll(zs[g], s, 1) if s else zs[g]
-                    p = w[g // 4]
-                    w[g // 4] = v if p is None else jnp.where(lane16 < 32 * k, p, v)
-                send_t[4 * q + m, 0:16] = w[0].astype(BF16)
-                send_t[4 * q + m, 16:32] = w[1].astype(BF16)
+                w = None
+                for i in range(3):
+                    s = (32 * (i - m)) % 128
+                    v = pltpu.roll(zs[i], s, 1) if s else zs[i]
+                    w = v if w is None else jnp.where(lane16 < 32 * i, w, v)
+                send_t[e, 4 * q + m] = w.astype(BF16)
             return 0
 
         lax.fori_loop(0, 8, body, 0)
 
     def offsets(half, dy):
-        turns = ((1, -1, 2, -2), (3, -3, 4, 0))[half]
-        return [(dy, dz) for dz in turns if dy or dz]
+        turns = ((3, -3, 4, -2), (2, 1, -1, 0))[half]
+        return [((2, 1, 3, 0)[dy], dz) for dz in turns if (2, 1, 3, 0)[dy] or dz]
 
     def group_ref(j):
         n = len(offsets(j % 2, j % 8 // 2))
-        return send.at[j // 8, pl.ds(0, n)] if j < 16 else send_t.at[pl.ds(0, n)]
+        return send.at[0, pl.ds(0, n)] if j < 16 else send_t.at[0, pl.ds(0, n)]
 
     def group_start(j):
         p = j // 8
@@ -165,7 +158,7 @@
             if p < 2:
                 src, dst = send.at[p, d], recv.at[p, pl.ds(pl.multiple_of(ROWS * f, 16), ROWS)]
             else:
-                src, dst = send_t.at[d], recv_t.at[f]
+                src, dst = send_t.at[p - 2, d], recv_t.at[p - 2, f]
             pltpu.make_async_remote_copy(
                 src_ref=src, dst_ref=dst, send_sem=a2a_s.at[j], recv_sem=a2a_r.at[p],
                 device_id=(r, d), device_id_type=MESH,
@@ -174,26 +167,25 @@
     def group_wait(j):
         pltpu.make_async_copy(group_ref(j), group_ref(j), a2a_s.at[j]).wait()
 
-    started = [0]
-
-    def pump(upto):
-        for j in range(started[0], upto):
+    def groups_start(p, first, last):
+        for j in range(8 * p + first, 8 * p + last):
             group_start(j)
-        started[0] = max(started[0], upto)
 
     loads[0].wait()
     pack_main(0)
     pl.semaphore_wait(bar, N - 1 + R - 1)
-    pump(8)
+    groups_start(0, 0, 8)
+    pack_tail(0)
+    groups_start(2, 0, 8)
     loads[1].wait()
     pack_main(1)
+    groups_start(1, 0, 8)
+    pack_tail(1)
     for c in loads[6:]:
         c.start()
-    pump(16)
-    pack_tail()
     for e in range(2):
         recv[e, pl.ds(pl.multiple_of(ROWS * f, 16), ROWS)] = send[e, f]
-    recv_t[f] = send_t[f]
+        recv_t[e, f] = send_t[e, f]
 
     loads[4].wait()
     loads[5].wait()
@@ -238,11 +230,16 @@
     kk = lax.broadcasted_iota(I32, (SPAN, 128), 0).astype(F32)
     first_a, first_b = div(5 * block_of[0], 4), div(5 * block_of[1], 4)
     first_a = jnp.minimum(first_a, 13)
-    tails = [b + 1 + div(b, 4) for b in (mine_first, rem(mine_first, 4) + 8)]
-    for s, g in enumerate((first_a, first_a + 1, first_b, first_b + 1, tails[0], tails[1])):
+    tail_a = block_of[0] + 1 + div(block_of[0], 4)
+    def fill(to, g):
         hot = jnp.where(kk == merged[pl.ds(g, 1), :], 1.0, 0.0).astype(BF16)
-        basis[s, :, 0:128] = dot(cos_v[2], hot).astype(BF16)
-        basis[s, :, 128:256] = dot(cos_v[3], hot).astype(BF16)
+        to[:, 0:128] = dot(cos_v[2], hot).astype(BF16)
+        to[:, 128:256] = dot(cos_v[3], hot).astype(BF16)
+
+    for s, g in enumerate((first_a, first_a + 1, first_b, first_b + 1, tail_a)):
+        fill(basis.at[s], g)
+    for c in range(6):
+        fill(basis_last.at[c], c + 7 + (c + 6) // 4)
 
     loads[3].wait()
 
@@ -258,11 +255,13 @@
             axis=0,
         )
 
+    TAIL_BLOCKS = ((0, 1, 2, 3), (4, 5), (6, 7, 8, 9), (10, 11))
+
     def err_columns(tb):
         return jnp.concatenate(
             [
-                e_v[(4 * tb + j) // 6, 128:160, SPAN * ((4 * tb + j) % 6):SPAN * ((4 * tb + j) % 6) + SPAN]
-                for j in range(4)
+                e_v[b // 6, 128:160, SPAN * (b % 6):SPAN * (b % 6) + SPAN]
+                for b in TAIL_BLOCKS[tb] + TAIL_BLOCKS[tb][:4 - len(TAIL_BLOCKS[tb])]
             ],
             axis=0,
         )
@@ -272,8 +271,8 @@
         return low[32 * ga:32 * ga + 64]
 
     def tail_rows(tb):
-        base = 32 * (5 * tb + 1)
-        return low[base:base + 128]
+        gs = [b + 1 + b // 4 for b in TAIL_BLOCKS[tb]]
+        return jnp.concatenate([low[32 * g:32 * g + 32] for g in gs], axis=0)
 
     def main_select(b, o):
         pa, pb = o[0:16] + o[16:32], o[32:48] + o[48:64]
@@ -281,17 +280,17 @@
 
     def tail_select(o):
         p = o[0:16] + o[16:32]
-        for j in range(1, 4):
+        for j in range(1, o.shape[0] // 32):
             p = jnp.where(lane16 < 32 * j, p, o[32 * j:32 * j + 16] + o[32 * j + 16:32 * j + 32])
         return p
 
     for b in range(12):
         from_err[b] = 0.95 * main_select(b, dot_nt(main_rows(b), turned(b // 6, b % 6)))
-    for tb in range(3):
+    for tb in range(4):
         from_err[12 + tb] = 0.95 * tail_select(dot_nt(tail_rows(tb), err_columns(tb)))
 
     def take_delta(p):
-        part = recv.at[p, pl.ds(0, (N - 1) * ROWS)] if p < 2 else recv_t.at[pl.ds(0, N - 1)]
+        part = recv.at[p, pl.ds(0, (N - 1) * ROWS)] if p < 2 else recv_t.at[p - 2, pl.ds(0, N - 1)]
         pltpu.make_async_copy(part, part, a2a_r.at[p]).wait()
 
     def pick_main(e):
@@ -301,20 +300,20 @@
             x = recv[e, SPAN * c:SPAN * c + SPAN]
             kept[b] = (main_select(b, dot(main_rows(b), x)) + from_err[b]).astype(BF16)
 
-    def pick_tail():
-        take_delta(2)
-        for tb in range(3):
+    def pick_tail(e):
+        take_delta(2 + e)
+        for tb in (2 * e, 2 * e + 1):
             for t16 in range(16):
                 v = None
-                for j in range(4):
-                    b = 4 * tb + j
-                    e, row = b // 6, SPAN * (b % 6) + 16 * t16
-                    s, g = row // ROWS, 3 * e + (row % ROWS) // 16
-                    w = recv_t[s, 16 * (g // 4):16 * (g // 4) + 16].astype(F32)
-                    sh = (32 * (j - g)) % 128
+                for j, b in enumerate(TAIL_BLOCKS[tb]):
+                    row = SPAN * (b % 6) + 16 * t16
+                    i = (row % ROWS) // 16
+                    w = recv_t[e, row // ROWS].astype(F32)
+                    sh = (32 * (j - i)) % 128
                     w = pltpu.roll(w, sh, 1) if sh else w
                     v = w if v is None else jnp.where(lane16 < 32 * j, v, w)
                 x_t[tb, 16 * t16:16 * t16 + 16] = v.astype(BF16)
+        for tb in (2 * e, 2 * e + 1):
             kept[12 + tb] = (tail_select(dot(tail_rows(tb), x_t[tb])) + from_err[12 + tb]).astype(BF16)
 
     def tile_of(slot, b8):
@@ -322,7 +321,7 @@
             return jnp.minimum(b8, 5)
         if slot == 1:
             return jnp.where(b8 < 4, b8 + 8, jnp.maximum(b8, 6))
-        return 12 + div(b8, 4) if slot == 2 else 14
+        return jnp.where(b8 < 4, 12, 13)
 
     def send_kept(slot):
         rows = pl.ds(pl.multiple_of(16 * r, 16), 16)
@@ -335,6 +334,54 @@
         pltpu.make_async_copy(
             kept.at[tile_of(slot, mine_first)], kept_in.at[slot, rows], kept_r.at[slot]
         ).start()
+
+    def send_last():
+        rows = pl.ds(pl.multiple_of(16 * r, 16), 16)
+        for o in (4, 3, 5, 2, 6, 1, 7):
+            pltpu.make_async_remote_copy(
+                src_ref=kept.at[pl.ds(14, 2)], dst_ref=kept_last.at[:, rows],
+                send_sem=kept_s.at[3], recv_sem=kept_r.at[3],
+                device_id=(rem(r + o, R), f), device_id_type=MESH,
+            ).start()
+        for k in range(2):
+            kept_last[k, rows] = kept[14 + k]
+
+    def average_last():
+        part = kept_last.at[:, pl.ds(0, 16 * (R - 1))]
+        pltpu.make_async_copy(part, part, kept_r.at[3]).wait()
+        into, outof = lax.broadcasted_iota(I32, (128, 128), 0), lanes((128, 128))
+        ks = []
+        for c in range(6):
+            same = (div(into, 32) == c % 4) & (rem(into, 32) == rem(outof, 32))
+            ks.append(dot(kept_last[c // 4], jnp.where(same, 1.0, 0.0).astype(BF16)).astype(BF16))
+        for c in range(6):
+            u_last[SPAN * c:SPAN * c + SPAN] = (
+                dot(basis_last[c], jnp.concatenate([ks[c], ks[c]], axis=0)) * 0.125
+            ).astype(BF16)
+        for d in range(N):
+            w = [u_last[ROWS * d + 16 * i:ROWS * d + 16 * i + 16] for i in range(3)]
+            last_msg[d] = jnp.where(lane16 < 32, w[0], jnp.where(lane16 < 64, w[1], w[2]))
+        for dy in (2, 1, 3, 0):
+            for dz in (4, 3, -3, 2, -2, 1, -1, 0):
+                if dy or dz:
+                    d = 8 * rem(y + dy, 4) + rem(z + dz + 8, 8)
+                    pltpu.make_async_remote_copy(
+                        src_ref=last_msg.at[d], dst_ref=last_recv.at[f], send_sem=last_s, recv_sem=last_r,
+                        device_id=(r, d), device_id_type=MESH,
+                    ).start()
+        last_recv[f] = last_msg[f]
+
+    def take_last():
+        part = last_recv.at[pl.ds(0, N - 1)]
+        pltpu.make_async_copy(part, part, last_r).wait()
+        for q in range(8):
+            ws = [last_recv[4 * q + m].astype(F32) for m in range(4)]
+            for i in range(3):
+                v = None
+                for m in range(4):
+                    w = pltpu.roll(ws[m], (32 * (m - i)) % 128, 1) if m != i else ws[m]
+                    v = w if v is None else jnp.where(lane16 < 32 * m, v, w)
+                last_tail[q, 16 * i:16 * i + 16] = v.astype(BF16)
 
     def restore_main(e):
         for c in range(6):
@@ -350,18 +397,18 @@
                     e, pl.ds(pl.multiple_of(32 * rem(i - fm + 4, 4), 32), 32), SPAN * c:SPAN * c + SPAN
                 ] = en[32 * i:32 * i + 32]
 
-    def restore_tail():
-        for tb in range(3):
+    def restore_tail(e):
+        for tb in (2 * e, 2 * e + 1):
             k, zero = kept[12 + tb], jnp.zeros((16, 128), BF16)
             ks = []
-            for j in range(4):
+            for j in range(len(TAIL_BLOCKS[tb])):
                 kj = jnp.where((lane16 >= 32 * j) & (lane16 < 32 * j + 32), k, zero)
                 ks += [kj, kj]
             back = dot_tn(jnp.concatenate(ks, axis=0), tail_rows(tb))
             en = 0.95 * err_columns(tb).astype(F32) + jnp.transpose(x_t[tb].astype(F32)) - back
             en = en.astype(BF16)
-            for j in range(4):
-                e, c = (4 * tb + j) // 6, (4 * tb + j) % 6
+            for j, b in enumerate(TAIL_BLOCKS[tb]):
+                c = b % 6
                 err_out[e, 128:160, SPAN * c:SPAN * c + SPAN] = en[32 * j:32 * j + 32]
 
     def when(flag, body):
@@ -371,15 +418,15 @@
             pl.when(flag)(body)
 
     def upd_move(s, v, n, what):
-        b = block_of[s]
-        e, c = div(b, 6), rem(b, 6)
+        e = s % 2
+        c = block_of[e] - 6 * e
         at, to, rows = PIECES[v][n]
         d = 16 * div(c, 3) + 5 * v + n
         if s < 2:
             src, dst = u_out.at[s, pl.ds(at, rows)], upd.at[s, r, y, pl.ds(to, rows)]
         else:
-            src, dst = u_msg.at[s - 2, n], u_recv.at[1 if to else 0, e, y]
-        arrived = upd_r.at[min(s, 2)]
+            src, dst = u_msg.at[e, n], u_recv.at[e, 1 if to else 0, y]
+        arrived = upd_r.at[s]
 
         @pl.when(d != f)
         def _():
@@ -396,7 +443,7 @@
 
     def upd_all(s, what):
         for v in range(3):
-            @pl.when(rem(rem(block_of[s], 6), 3) == v)
+            @pl.when(rem(block_of[s % 2], 3) == v)
             def _():
                 for n in range(6):
                     upd_move(s, v, n, what)
@@ -416,25 +463,22 @@
         u_out[s] = (u * 0.125).astype(BF16)
         when(has_block[s], functools.partial(upd_all, s, "start"))
 
-    def average_tail():
+    def average_tail(e):
         into, outof = lax.broadcasted_iota(I32, (128, 128), 0), lanes((128, 128))
-        same = (div(into, 32) == rem(mine_first, 4)) & (rem(into, 32) == rem(outof, 32))
+        same = (div(into, 32) == rem(block_of[e] + 2 * e, 4)) & (rem(into, 32) == rem(outof, 32))
         same = jnp.where(same, 1.0, 0.0).astype(BF16)
-        ks = [dot(take_kept(s), same).astype(BF16) for s in (2, 3)]
-        for s in (2, 3):
-            k = ks[s - 2]
-            u_tail[s - 2] = dot(basis[2 + s], jnp.concatenate([k, k], axis=0)) * 0.125
-        for s in (2, 3):
-            for v in range(3):
-                @pl.when(rem(rem(block_of[s], 6), 3) == v)
-                def _():
-                    for n, (at, to, rows) in enumerate(PIECES[v]):
-                        w = None
-                        for i in range(rows // 16):
-                            x = u_tail[s - 2, at + 16 * i:at + 16 * i + 16]
-                            w = x if w is None else jnp.where(lane16 < to * 2 + 32 * i, w, x)
-                        u_msg[s - 2, n] = w.astype(BF16)
-            when(has_block[s], functools.partial(upd_all, s, "start"))
+        k = dot(take_kept(2 + e), same).astype(BF16)
+        u_tail[...] = dot(basis[4 + e], jnp.concatenate([k, k], axis=0)) * 0.125
+        for v in range(3):
+            @pl.when(rem(block_of[e], 3) == v)
+            def _():
+                for n, (at, to, rows) in enumerate(PIECES[v]):
+                    w = None
+                    for i in range(rows // 16):
+                        x = u_tail[at + 16 * i:at + 16 * i + 16]
+                        w = x if w is None else jnp.where(lane16 < to * 2 + 32 * i, w, x)
+                    u_msg[e, n] = w.astype(BF16)
+        when(has_block[e], functools.partial(upd_all, 2 + e, "start"))
 
     chunk = [div(3 * f + i, 16) for i in range(3)]
 
@@ -448,11 +492,11 @@
 
         @pl.when(chunk[0] == chunk[2])
         def _():
-            some(u_recv.at[0])
+            some(u_recv.at[p - 2, 0])
 
         @pl.when(chunk[0] != chunk[2])
         def _():
-            some(u_recv)
+            some(u_recv.at[p - 2])
 
     def fwd_copy(p, other):
         ref = upd.at[p, r] if p < 2 else upd_tail.at[r]
@@ -463,57 +507,64 @@
 
     def forward(p):
         wait_upd(p)
-        if p == 2:
-            for e in range(2):
-                for i in range(3):
-                    whole = jnp.zeros((16, 128), F32)
-                    behind = div(rem(r - 6 * e - chunk[i] + 2 * R, R), 2)
-                    for yy in range(4):
-                        m = rem(behind - yy + 4, 4)
-                        v = u_recv[chunk[i] - chunk[0], e, yy].astype(F32)
-                        v = pltpu.roll(v, rem(32 * (m - i) + 128, 128), 1)
-                        whole = jnp.where(div(lane16, 32) == m, v, whole)
-                    upd_tail[r, ROWS * e + 16 * i:ROWS * e + 16 * i + 16] = whole.astype(BF16)
+        if p >= 2:
+            e = p - 2
+            for i in range(3):
+                whole = jnp.zeros((16, 128), F32)
+                behind = div(rem(r - 6 * e - chunk[i] + 2 * R, R), 2)
+                for yy in range(4):
+                    m = rem(behind - yy + 4, 4)
+                    v = u_recv[e, chunk[i] - chunk[0], yy].astype(F32)
+                    v = pltpu.roll(v, rem(32 * (m - i) + 128, 128), 1)
+                    whole = jnp.where(div(lane16, 32) == m, v, whole)
+                upd_tail[r, 16 * i:16 * i + 16] = whole.astype(BF16)
         for o in range(1, R):
             fwd_copy(p, rem(r + o, R)).start()
 
     pick_main(0)
     send_kept(0)
+    pick_tail(0)
+    send_kept(2)
     restore_main(0)
-    pump(20)
+    restore_tail(0)
     average_main(0)
-    pump(24)
+    average_tail(0)
+    groups_start(3, 0, 8)
     pick_main(1)
     send_kept(1)
+    average_main(1)
+    pick_tail(1)
+    send_last()
     forward(0)
+    forward(2)
     restore_main(1)
-    average_main(1)
-    pick_tail()
-    send_kept(2)
-    send_kept(3)
-    average_tail()
+    average_last()
     forward(1)
-    restore_tail()
-    forward(2)
+    restore_tail(1)
+    take_last()
 
     for p in range(3):
         part = upd.at[p, pl.ds(0, R - 1)] if p < 2 else upd_tail.at[pl.ds(0, R - 1)]
         pltpu.make_async_copy(part, part, fwd_r.at[p]).wait()
         pltpu.make_async_copy(part, part, fwd_s.at[p]).wait()
 
-    for j in range(24):
+    for j in range(32):
         group_wait(j)
     for c in loads[6:]:
         c.wait()
 
     part = idx_all.at[pl.ds(0, R - 1)]
     pltpu.make_async_copy(part, part, idx_s).wait()
-    for s in range(4):
+    for s in range(3):
         pltpu.make_async_copy(
             kept_in.at[s, pl.ds(0, 16 * (R - 1))], kept_in.at[s, pl.ds(0, 16 * (R - 1))], kept_s.at[s]
         ).wait()
-    for s in range(4):
-        when(has_block[s], functools.partial(upd_all, s, "wait"))
+    for s in range(3):
+        when(has_block[s % 2], functools.partial(upd_all, s, "wait"))
+    part = kept_last.at[:, pl.ds(0, 16 * (R - 1))]
+    pltpu.make_async_copy(part, part, kept_s.at[3]).wait()
+    part = last_msg.at[pl.ds(0, N - 1)]
+    pltpu.make_async_copy(part, part, last_s).wait()
 
 
 def exchange(delta, err, cos, idx, count, theta, momentum):
@@ -525,13 +576,14 @@
         exchange_kernel,
         out_shape=(
             pltpu.VMEM((2, R, 4, ROWS, 128), BF16),
-            pltpu.VMEM((R, 2 * ROWS, 128), BF16),
+            pltpu.VMEM((R, ROWS, 128), BF16),
+            pltpu.VMEM((8, ROWS, 128), BF16),
             pltpu.VMEM((2, 160, 1536), BF16),
             pltpu.VMEM(theta.shape, F32),
             pltpu.VMEM(theta.shape, F32),
         ),
         in_specs=[hbm] * 7,
-        out_specs=(vmem,) * 5,
+        out_specs=(vmem,) * 6,
         scratch_shapes=[
             pltpu.VMEM((2, ROWS, 5120), BF16),
             pltpu.VMEM((2, 160, 1536), BF16),
@@ -542,32 +594,39 @@
             pltpu.VMEM((16, 128), F32),
             pltpu.VMEM((16, 128), F32),
             pltpu.VMEM((2, N, ROWS, 128), BF16),
-            pltpu.VMEM((N, 32, 128), BF16),
+            pltpu.VMEM((2, N, 16, 128), BF16),
             pltpu.VMEM((2, N * ROWS, 128), BF16),
-            pltpu.VMEM((N, 32, 128), BF16),
-            pltpu.VMEM((3, SPAN, 128), BF16),
+            pltpu.VMEM((2, N, 16, 128), BF16),
+            pltpu.VMEM((4, SPAN, 128), BF16),
             pltpu.VMEM((15 * 32, SPAN), BF16),
             pltpu.VMEM((6, SPAN, SPAN), BF16),
-            pltpu.VMEM((15, 16, 128), F32),
+            pltpu.VMEM((16, 16, 128), F32),
             pltpu.VMEM((R, 16, 128), F32),
             pltpu.VMEM((16, 128), F32),
-            pltpu.VMEM((15, 16, 128), BF16),
+            pltpu.VMEM((16, 16, 128), BF16),
             pltpu.VMEM((4, 128, 128), BF16),
             pltpu.VMEM((2, SPAN, 128), BF16),
-            pltpu.VMEM((2, SPAN, 128), F32),
+            pltpu.VMEM((SPAN, 128), F32),
             pltpu.VMEM((2, 6, 16, 128), BF16),
             pltpu.VMEM((2, 2, 4, 16, 128), BF16),
+            pltpu.VMEM((2, 128, 128), BF16),
+            pltpu.VMEM((6, SPAN, SPAN), BF16),
+            pltpu.VMEM((N * ROWS, 128), BF16),
+            pltpu.VMEM((N, 16, 128), BF16),
+            pltpu.VMEM((N, 16, 128), BF16),
             pltpu.SemaphoreType.DMA((8,)),
-            pltpu.SemaphoreType.DMA((24,)),
-            pltpu.SemaphoreType.DMA((3,)),
+            pltpu.SemaphoreType.DMA((32,)),
+            pltpu.SemaphoreType.DMA((4,)),
             pltpu.SemaphoreType.DMA,
             pltpu.SemaphoreType.DMA,
             pltpu.SemaphoreType.DMA((4,)),
             pltpu.SemaphoreType.DMA((4,)),
             pltpu.SemaphoreType.DMA((4, 6)),
-            pltpu.SemaphoreType.DMA((3,)),
-            pltpu.SemaphoreType.DMA((3,)),
-            pltpu.SemaphoreType.DMA((3,)),
+            pltpu.SemaphoreType.DMA((4,)),
+            pltpu.SemaphoreType.DMA((4,)),
+            pltpu.SemaphoreType.DMA((4,)),
+            pltpu.SemaphoreType.DMA,
+            pltpu.SemaphoreType.DMA,
         ],
         compiler_params=pltpu.CompilerParams(
             collective_id=0, has_side_effects=True, vmem_limit_bytes=32 << 20
@@ -577,7 +636,7 @@
 
 
 def finish_kernel(
-    upd, upd_tail, err, theta, momentum,
+    upd, upd_tail, last_tail, err, theta, momentum,
     theta_out, momentum_out, err_out,
     th, mo, err_sem, th_sem, mo_sem,
 ):
@@ -601,10 +660,10 @@
                 shift = 6 * e + div(3 * f + i, 16) + core
                 reps = [rem(shift + 2 * ((y + m) % 4), R) for m in range(4)]
                 main = [upd[e, reps[m], y, rows].astype(F32) for m in range(4)]
-                tail = [
-                    upd_tail[reps[m], ROWS * e + 16 * i:ROWS * e + 16 * i + 16].astype(F32)
-                    for m in range(4)
-                ]
+                if e == 0:
+                    tail = [upd_tail[reps[m], rows].astype(F32) for m in range(4)]
+                else:
+                    tail = [last_tail[q, rows].astype(F32)] * 4
                 tiles = [
                     main[0],
                     jnp.where(lane < 32, tail[0], main[1]),
@@ -628,7 +687,7 @@
 def finish(*args):
     vmem = pl.BlockSpec(memory_space=pltpu.VMEM)
     hbm = pl.BlockSpec(memory_space=pltpu.HBM)
-    upd, upd_tail, err, theta, momentum = args
+    err, theta = args[3], args[4]
     args = [pltpu.with_memory_space_constraint(a, pltpu.VMEM) for a in args]
     return pl.pallas_call(
         finish_kernel,
@@ -637,7 +696,7 @@
             jax.ShapeDtypeStruct(theta.shape, F32),
             jax.ShapeDtypeStruct(err.shape, BF16),
         ),
-        in_specs=[vmem] * 5,
+        in_specs=[vmem] * 6,
         out_specs=(hbm, hbm, hbm),
         scratch_shapes=[
             pltpu.VMEM((2, ROWS, 5120), F32),

time: 57.5 us -> 55.7 us (0.969)
  Pallas kernels: 56.7 us -> 54.9 us
    pallas_call x1, Pallas kernels: 54.2 us -> 52.5 us  [exchange(): pl.pallas_call(exchange_kernel, out_shape=(pltpu.VMEM((2, R, 4, ROWS, 128...]
where the time goes in v3:
time: 55.7 us; the launch traced here: 55.6 us
  Pallas kernels  54.9 us (99%)
  between operations  0.64 us (1%)
    pallas_call x1, Pallas kernels, exchange(): pl.pallas_call(exchange_kernel, out_shape=(pltpu.VMEM((2, R, 4, ROWS, 128...  52.5 us
    pallas_call x1, Pallas kernels, finish(): pl.pallas_call(finish_kernel, out_shape=(jax.ShapeDtypeStruct(theta.shape...  2.49 us

profile of v3, /device:TPU:1, one launch (start us, length us, event | category | flops | bytes accessed | tf_op | source)
XLA Modules:
  0.0 55.6 jit_solution(15394535010776264514)
XLA Ops:
  0.6 52.5 %exchange.1 = (bf16[2,8,4,48,128]{4,3,2,1,0:T(8,128)(2,1)S(1)}, bf16[8,48,128]{2,1,0:T(8,128)(2,1)S(1)}, bf16[8,48,128]{2,1,0:T(8,128)(2,1)S(1)}, bf16[2,160,153...) custom-call(bf16[2,48,5120]{2,1,0:T(8,128)(2,1)} %bitcast.8, ...), custom_call_target="tpu_custom_call" | custom-call | tf_op jit(solution)/shard_map/exchange/pallas_call | solution.py:575
  53.1 2.5 %finish.1 = (f32[2,48,5120]{2,1,0:T(8,128)}, f32[2,48,5120]{2,1,0:T(8,128)}, bf16[2,160,1536]{2,1,0:T(8,128)(2,1)}) custom-call(bf16[2,8,4,48,128]{4,3,2,1,0:T(8,128)(2,1)S(1)} %get-tuple-element.12.upd, bf16[8,48,128]{2,1,0:T(8,128)(2,1)S(1)} %get-tuple-element.13.upd_tail, bf16[8,48,128]{2,1,0:T(8,128)(2,1)S(1)} %get-tuple-element.14.last_tail, ...), custom_call_target="tpu_custom_call" | custom-call | tf_op jit(solution)/shard_map/finish/pallas_call | solution.py:692

commit v4 on v3

--- a/solution.py
+++ b/solution.py
@@ -527,9 +527,9 @@
     send_kept(2)
     restore_main(0)
     restore_tail(0)
+    groups_start(3, 0, 8)
     average_main(0)
     average_tail(0)
-    groups_start(3, 0, 8)
     pick_main(1)
     send_kept(1)
     average_main(1)

time: 55.7 us -> 55.2 us (level)
  no operation moved by 1% of the time
where the time goes in v4:
time: 55.2 us; the launch traced here: 55.1 us
  Pallas kernels  54.5 us (99%)
  between operations  0.64 us (1%)
    pallas_call x1, Pallas kernels, exchange(): pl.pallas_call(exchange_kernel, out_shape=(pltpu.VMEM((2, R, 4, ROWS, 128...  52 us
    pallas_call x1, Pallas kernels, finish(): pl.pallas_call(finish_kernel, out_shape=(jax.ShapeDtypeStruct(theta.shape...  2.49 us

profile of v4, /device:TPU:1, one launch (start us, length us, event | category | flops | bytes accessed | tf_op | source)
XLA Modules:
  0.0 55.1 jit_solution(13109701538733714461)
XLA Ops:
  0.6 52.0 %exchange.1 = (bf16[2,8,4,48,128]{4,3,2,1,0:T(8,128)(2,1)S(1)}, bf16[8,48,128]{2,1,0:T(8,128)(2,1)S(1)}, bf16[8,48,128]{2,1,0:T(8,128)(2,1)S(1)}, bf16[2,160,153...) custom-call(bf16[2,48,5120]{2,1,0:T(8,128)(2,1)} %bitcast.8, ...), custom_call_target="tpu_custom_call" | custom-call | tf_op jit(solution)/shard_map/exchange/pallas_call | solution.py:575
  52.6 2.5 %finish.1 = (f32[2,48,5120]{2,1,0:T(8,128)}, f32[2,48,5120]{2,1,0:T(8,128)}, bf16[2,160,1536]{2,1,0:T(8,128)(2,1)}) custom-call(bf16[2,8,4,48,128]{4,3,2,1,0:T(8,128)(2,1)S(1)} %get-tuple-element.12.upd, bf16[8,48,128]{2,1,0:T(8,128)(2,1)S(1)} %get-tuple-element.13.upd_tail, bf16[8,48,128]{2,1,0:T(8,128)(2,1)S(1)} %get-tuple-element.14.last_tail, ...), custom_call_target="tpu_custom_call" | custom-call | tf_op jit(solution)/shard_map/finish/pallas_call | solution.py:692
